TPU v7x, 1024 devices: a whole 8x8x8 slice. The times are simulated.
1024 devices in a mesh: wide: 16 (over x, core), tp: 64 (over z, y).
Axes of the slice: x: 8, y: 8, z: 8, core: 2. Of those that a mesh axis runs over, the one named last changes fastest.
Arguments:
- queries: bfloat16 [16, 64, 192, 1024], P('wide', 'tp')
- own_kv: bfloat16 [2, 16, 64, 192, 128], P(None, 'wide', 'tp'), may hold values from -6 to 6
- doc_kv: bfloat16 [2, 32, 128, 1024], P(None, 'wide', 'tp'), may hold values from -6 to 6
- doc_lengths: int32 [32], replicated, may hold values from 16 to 128, as said below
- doc_ids: int32 [128, 8], replicated, may hold values from 0 to 31, as said below
- d_out: bfloat16 [16, 64, 192, 1024], P('wide', 'tp'), may hold values from -6 to 6
Outputs:
- attended: bfloat16 [16, 64, 192, 1024], P('wide', 'tp')
- d_queries: bfloat16 [16, 64, 192, 1024], P('wide', 'tp')
- d_doc_kv: float32 [2, 32, 128, 1024], P(None, 'wide', 'tp')
Inputs may be any that keep to these rules, and one draw needn't show every extreme that they name: `doc_ids`: each row names 8 documents whose owners, document // 2, are all different. `doc_lengths`: the longest document fills its whole block.
All inputs are finite; a program needn't handle non-finite values.
Results may differ from a plain program's by a relative error of at most 0.028.
Values may be sent and summed in bfloat16 or wider, within the bound.
No kernel may reach another device: no remote copies, remote signals or barrier semaphores. Data moves between devices by JAX's collectives and lax.ppermute only.
A program may use at most 32 MiB of HBM per device.

v0:
```python
import functools
import math

import jax
import jax.numpy as jnp
from jax import lax
from jax.experimental import pallas as pl
from jax.experimental.pallas import tpu as pltpu
from jax.sharding import PartitionSpec as P

NT = (((1,), (1,)), ((), ()))
NN = (((1,), (0,)), ((), ()))
TN = (((0,), (0,)), ((), ()))
OUT_OF_REACH = -2e38
STACK = 4


def dot(a, b, dims):
    return lax.dot_general(a, b, dims, preferred_element_type=jnp.float32)


def attention_kernel(heads, uses, q_ref, g_ref, own_ref, limit_ref, doc_ref, att_ref, dq_ref, dkv_ref, dk_sum, dv_sum):
    low = jnp.bfloat16
    sources, _, per_source, head_dim = doc_ref.shape
    slots = sources * per_source
    rows = q_ref.shape[0]
    scale = 1.0 / math.sqrt(head_dim)
    exponent = scale * math.log2(math.e)
    doc_k = doc_ref[:, 0].reshape(slots, head_dim)
    doc_v = doc_ref[:, 1].reshape(slots, head_dim)
    own_k, own_v = own_ref[0], own_ref[1]
    token = lax.broadcasted_iota(jnp.int32, (1, slots), 1) // uses
    doc_allowed = token < limit_ref[...]
    causal = lax.broadcasted_iota(jnp.int32, (rows, rows), 1) <= lax.broadcasted_iota(
        jnp.int32, (rows, rows), 0
    )
    causal = jnp.concatenate([causal.astype(jnp.int32)] * STACK, axis=0) > 0

    def stacked(ref, first):
        return jnp.concatenate(
            [ref[:, pl.ds((first + h) * head_dim, head_dim)] for h in range(STACK)], axis=0
        )

    def unstack(ref, first, value):
        for h in range(STACK):
            ref[:, pl.ds((first + h) * head_dim, head_dim)] = value[h * rows : (h + 1) * rows]

    for first in range(0, heads, STACK):
        q, g = stacked(q_ref, first), stacked(g_ref, first)
        s_doc = jnp.where(doc_allowed, dot(q, doc_k, NT), OUT_OF_REACH)
        s_own = jnp.where(causal, dot(q, own_k, NT), OUT_OF_REACH)
        top = jnp.maximum(
            jnp.max(s_doc, axis=1, keepdims=True), jnp.max(s_own, axis=1, keepdims=True)
        )
        e_doc = jnp.exp2((s_doc - top) * exponent)
        e_own = jnp.exp2((s_own - top) * exponent)
        total = jnp.sum(e_doc, axis=1, keepdims=True) + jnp.sum(e_own, axis=1, keepdims=True)
        inverse = 1.0 / total
        w_doc, w_own = e_doc * inverse, e_own * inverse
        w_doc_low, w_own_low = w_doc.astype(low), w_own.astype(low)
        att = (dot(w_doc_low, doc_v, NN) + dot(w_own_low, own_v, NN)).astype(low)
        row_dot = jnp.sum(
            g.astype(jnp.float32) * att.astype(jnp.float32), axis=1, keepdims=True
        )
        ds_doc = (w_doc * (dot(g, doc_v, NT) - row_dot)).astype(low)
        ds_own = (w_own * (dot(g, own_v, NT) - row_dot)).astype(low)
        dq = ((dot(ds_doc, doc_k, NN) + dot(ds_own, own_k, NN)) * scale).astype(low)
        unstack(att_ref, first, att)
        unstack(dq_ref, first, dq)
        dk, dv = dot(q.T, ds_doc, NN), dot(g.T, w_doc_low, NN)
        if first:
            dk, dv = dk_sum[...] + dk, dv_sum[...] + dv
        if first + STACK < heads:
            dk_sum[...] = dk
            dv_sum[...] = dv
        else:
            dkv_ref[:, 0] = (dk.T * scale).astype(low).reshape(sources, per_source, head_dim)
            dkv_ref[:, 1] = dv.T.astype(low).reshape(sources, per_source, head_dim)


def attention(q, g, own, limits, docs, uses):
    rows, width = q.shape
    head_dim = own.shape[2]
    heads = width // head_dim
    slots = limits.shape[1]
    vmem = pl.BlockSpec(memory_space=pltpu.VMEM)
    return pl.pallas_call(
        functools.partial(attention_kernel, heads, uses),
        out_shape=(
            jax.ShapeDtypeStruct(q.shape, jnp.bfloat16),
            jax.ShapeDtypeStruct(q.shape, jnp.bfloat16),
            jax.ShapeDtypeStruct(docs.shape, jnp.bfloat16),
        ),
        in_specs=[vmem] * 5,
        out_specs=(vmem,) * 3,
        scratch_shapes=[pltpu.VMEM((head_dim, slots), jnp.float32)] * 2,
        compiler_params=pltpu.CompilerParams(vmem_limit_bytes=48 * 1024 * 1024),
        cost_estimate=pl.CostEstimate(
            flops=12 * heads * rows * (slots + rows) * head_dim,
            bytes_accessed=4 * 2 * q.size + 2 * 2 * docs.size,
            transcendentals=heads * rows * (slots + rows),
        ),
    )(q, g, own, limits, docs)


def select_kernel(reads_ref, every_ref, out_ref, rows_ref):
    owners, per_owner, head_dim = every_ref.shape
    subs, kv_heads, _, per_piece, _ = out_ref.shape
    docs_here = reads_ref.shape[1] // owners
    block_len = per_owner // (2 * docs_here * kv_heads)
    uses = per_piece // block_len
    rows_ref[...] = every_ref[...].astype(jnp.float32).reshape(owners * per_owner, head_dim)
    for kind in range(2):
        found = []
        for token in range(block_len):
            columns = []
            for h in range(kv_heads):
                of_head = [
                    rows_ref[pl.ds(((kind * docs_here + doc) * block_len + token) * kv_heads + h, owners, stride=per_owner), :]
                    for doc in range(docs_here)
                ]
                columns.append(jnp.concatenate(of_head, axis=0))
            table = jnp.concatenate(columns, axis=1).astype(jnp.bfloat16)
            found.append(dot(reads_ref[...], table, NN))
        for h in range(kv_heads):
            piece = [
                part[:, h * head_dim : (h + 1) * head_dim].reshape(subs, uses, head_dim)
                for part in found
            ]
            out_ref[:, h, kind] = jnp.concatenate(piece, axis=1).astype(jnp.bfloat16)


def select(reads, every, subs, kv_heads, per_piece):
    owners, per_owner, head_dim = every.shape
    vmem = pl.BlockSpec(memory_space=pltpu.VMEM)
    return pl.pallas_call(
        select_kernel,
        out_shape=jax.ShapeDtypeStruct((subs, kv_heads, 2, per_piece, head_dim), jnp.bfloat16),
        in_specs=[vmem] * 2,
        out_specs=vmem,
        scratch_shapes=[pltpu.VMEM((owners * per_owner, head_dim), jnp.float32)],
        compiler_params=pltpu.CompilerParams(vmem_limit_bytes=16 * 1024 * 1024),
        cost_estimate=pl.CostEstimate(
            flops=2 * reads.size * per_owner * head_dim,
            bytes_accessed=6 * every.size,
            transcendentals=0,
        ),
    )(reads, every)


def shards(queries, own_kv, doc_kv, doc_lengths, doc_ids, d_out):
    tp_width = lax.axis_size("tp")
    wide_width = lax.axis_size("wide")
    my_group = lax.axis_index("wide")
    head_dim = own_kv.shape[4]
    kv_heads = doc_kv.shape[3] // head_dim
    subs = tp_width // kv_heads
    my_sub = lax.axis_index("tp") // kv_heads
    docs_here, block_len = doc_kv.shape[1:3]
    uses = doc_ids.shape[1]
    slots = tp_width * block_len * uses

    slab = doc_kv.reshape(1, -1, head_dim)
    every = lax.all_to_all(
        jnp.broadcast_to(slab, (wide_width,) + slab.shape[1:]), "wide", 0, 0, tiled=True
    )
    doc_ids, doc_lengths, every = lax.optimization_barrier((doc_ids, doc_lengths, every))

    by_sub = lax.dynamic_index_in_dim(
        doc_ids.reshape(wide_width, subs, uses), my_group, 0, keepdims=False
    )
    order = jnp.arange(wide_width * docs_here, dtype=jnp.int32)
    order = order.reshape(wide_width, docs_here).T.reshape(-1)
    reads = (by_sub[:, :, None] == order).astype(jnp.bfloat16).reshape(subs * uses, -1)
    chosen = lax.dynamic_index_in_dim(by_sub, my_sub, 0, keepdims=False)
    lengths = jnp.sum(
        jnp.where(chosen[:, None] == jnp.arange(doc_lengths.shape[0], dtype=jnp.int32), doc_lengths, 0), axis=1
    )
    limits = jnp.tile(lengths, slots // uses)[None]

    picked = select(reads, every, subs, kv_heads, block_len * uses)
    picked = picked.reshape(tp_width, 2, block_len * uses, head_dim)
    picked, limits = lax.optimization_barrier((picked, limits))
    docs = lax.all_to_all(picked, "tp", 0, 0, tiled=True)

    attended, d_query, d_docs = attention(
        queries[0, 0], d_out[0, 0], own_kv[:, 0, 0], limits, docs, uses
    )

    back = lax.all_to_all(d_docs, "tp", 0, 0, tiled=True)
    back = back.reshape(subs, kv_heads, 2, block_len, uses, head_dim)
    by_doc = jnp.einsum(
        "zudw,zhktul->wkdthl",
        reads.reshape(subs, uses, docs_here, wide_width),
        back,
        preferred_element_type=jnp.float32,
    ).astype(jnp.bfloat16)
    by_doc = by_doc.reshape(wide_width, -1, head_dim)
    parts = lax.all_to_all(by_doc, "wide", 0, 0, tiled=True)
    d_doc = jnp.sum(parts.astype(jnp.float32), axis=0)
    d_doc = d_doc.reshape(2, docs_here, block_len, kv_heads * head_dim)
    return attended[None, None], d_query[None, None], d_doc


def solution(mesh):
    placed = (
        P("wide", "tp", None, None),
        P(None, "wide", "tp", None, None),
        P(None, "wide", "tp", None),
        P(),
        P(),
        P("wide", "tp", None, None),
    )
    return jax.shard_map(
        shards,
        mesh=mesh,
        in_specs=placed,
        out_specs=(
            P("wide", "tp", None, None),
            P("wide", "tp", None, None),
            P(None, "wide", "tp", None),
        ),
        check_vma=False,
    )
```

profile of v0, /device:TPU:1, one launch (start us, length us, event | category | flops | bytes accessed | tf_op | source)
XLA Modules:
  0.0 115.3 jit_solution(3167326060975755426)
XLA Ops:
  0.6 0.7 broadcast_in_dim.24
  1.4 0.8 broadcast_in_dim.25
  2.1 17.5 %all-to-all-start = ((bf16[16,64,128]{2,1,0:T(8,128)(2,1)}), bf16[16,64,128]{2,1,0:T(8,128)(2,1)S(1)}, u32[]{:S(2)}, u32[]{:S(2)}) async-start(bf16[16,64,128]{2,1,0:T(8,128)(2,1)} %broadcast_in_dim.25), calls=%async_computation | async-start | bytes 524288 | tf_op jit(solution)/shard_map/all_to_all | solution.py:164
  19.6 0.1 reshape.69
  19.7 11.8 %all-to-all-done.every_ref = bf16[16,64,128]{2,1,0:T(8,128)(2,1)S(1)} async-done(((bf16[16,64,128]{2,1,0:T(8,128)(2,1)}), bf16[16,64,128]{2,1,0:T(8,128)(2,1)S(1)}, u32[]{:S(2)}, u32[]{:S(2)}) %all-to-all-start) | async-done | bytes 262176 | tf_op jit(solution)/shard_map/all_to_all | solution.py:164
  31.5 0.0 copy-done.3
  31.5 0.1 copy.16
  31.6 0.1 eq.40
  31.7 0.6 copy-done.4
  32.3 0.2 select_reduce_fusion
  32.5 0.1 broadcast_in_dim_tile.3.limit_ref
  32.6 0.1 compare_convert_fusion.reads_ref
  32.7 0.5 shard_map.85
  33.2 0.0 copy-start.1
  33.2 0.0 copy-start.2
  33.2 31.9 %all_to_all.20.doc_ref = bf16[64,2,16,128]{3,2,1,0:T(8,128)(2,1)S(1)} all-to-all(bf16[64,2,16,128]{3,2,1,0:T(8,128)(2,1)S(1)} %bitcast.29), channel_id=1, replica_groups=mesh['wide'=16,'tp'=64] {'tp'}, dimensions={0} | all-to-all | bytes 1048576 | tf_op jit(solution)/shard_map/all_to_all | solution.py:184
  65.1 0.0 copy-done.1
  65.1 7.7 %shard_map.86 = (bf16[192,1024]{1,0:T(8,128)(2,1)}, bf16[192,1024]{1,0:T(8,128)(2,1)}, bf16[64,2,16,128]{3,2,1,0:T(8,128)(2,1)}) custom-call(bf16[192,1024]{1,0:T(8,128)(2,1)S(1)} %bitcast.30, bf16[192,1024]{1,0:T(8,128)(2,1)S(1)} %bitcast.31, bf16[2,192,128]{2,1,0:T(8,128)(2,1)S(1)} %bitcast.32, s32[1,1024]{1,0:T(1,128)S(1)} %broadcast_in_dim_tile.3.limit_ref, ...), custom_call_target="tpu_custom_call" | custom-call | flops 2868903936 | bytes 2621440 | tf_op jit(solution)/shard_map/pallas_call | solution.py:87
  72.9 6.4 %all-to-all-start.2 = ((bf16[64,2,16,128]{3,2,1,0:T(8,128)(2,1)}), bf16[64,2,16,128]{3,2,1,0:T(8,128)(2,1)S(1)}, u32[]{:S(2)}, u32[]{:S(2)}) async-start(bf16[64,2,16,128]{3,2,1,0:T(8,128)(2,1)} %get-tuple-element.18), calls=%async_computation.2 | async-start | bytes 1048576 | tf_op jit(solution)/shard_map/all_to_all | solution.py:190
  79.3 16.9 %all-to-all-done.2 = bf16[64,2,16,128]{3,2,1,0:T(8,128)(2,1)S(1)} async-done(((bf16[64,2,16,128]{3,2,1,0:T(8,128)(2,1)}), bf16[64,2,16,128]{3,2,1,0:T(8,128)(2,1)S(1)}, u32[]{:S(2)}, u32[]{:S(2)}) %all-to-all-start.2) | async-done | bytes 524320 | tf_op jit(solution)/shard_map/all_to_all | solution.py:190
  96.2 0.3 fusion.1
  96.6 0.2 copy.18
  96.7 17.8 %all_to_all.21 = bf16[16,64,128]{2,1,0:T(8,128)(2,1)S(1)} all-to-all(bf16[16,64,128]{2,1,0:T(8,128)(2,1)S(1)} %bitcast.34), channel_id=1, replica_groups=mesh['wide'=16,'tp'=64] {'wide'}, dimensions={0} | all-to-all | bytes 524288 | tf_op jit(solution)/shard_map/all_to_all | solution.py:199
  114.6 0.6 reshape.73
  (11 shorter events, 0.1 us)
Async XLA Ops:
  2.1 29.3 %all-to-all-start = ((bf16[16,64,128]{2,1,0:T(8,128)(2,1)}), bf16[16,64,128]{2,1,0:T(8,128)(2,1)S(1)}, u32[]{:S(2)}, u32[]{:S(2)}) async-start(bf16[16,64,128]{2,1,0:T(8,128)(2,1)} %broadcast_in_dim.25), calls=%async_computation | async-start | bytes 524288 | tf_op jit(solution)/shard_map/all_to_all | solution.py:164
  19.6 11.9 %copy-start.3 = (s32[128,8]{0,1:T(8,128)S(1)}, s32[128,8]{0,1:T(8,128)}, u32[]{:S(2)}) copy-start(s32[128,8]{0,1:T(8,128)} %param.10) | copy-start | bytes 12292
  31.7 0.7 copy-start.4
  33.2 31.9 %copy-start = (bf16[1,1,192,1024]{3,2,1,0:T(8,128)(2,1)S(1)}, bf16[1,1,192,1024]{3,2,1,0:T(8,128)(2,1)}, u32[]{:S(2)}) copy-start(bf16[1,1,192,1024]{3,2,1,0:T(8,128)(2,1)} %param.6) | copy-start | bytes 1179652
  33.2 31.9 %copy-start.1 = (bf16[1,1,192,1024]{3,2,1,0:T(8,128)(2,1)S(1)}, bf16[1,1,192,1024]{3,2,1,0:T(8,128)(2,1)}, u32[]{:S(2)}) copy-start(bf16[1,1,192,1024]{3,2,1,0:T(8,128)(2,1)} %param.11) | copy-start | bytes 1179652
  33.2 31.9 %copy-start.2 = (bf16[2,1,1,192,128]{4,3,2,1,0:T(8,128)(2,1)S(1)}, bf16[2,1,1,192,128]{4,3,2,1,0:T(8,128)(2,1)}, u32[]{:S(2)}) copy-start(bf16[2,1,1,192,128]{4,3,2,1,0:T(8,128)(2,1)} %param.7) | copy-start | bytes 294916
  72.9 23.3 %all-to-all-start.2 = ((bf16[64,2,16,128]{3,2,1,0:T(8,128)(2,1)}), bf16[64,2,16,128]{3,2,1,0:T(8,128)(2,1)S(1)}, u32[]{:S(2)}, u32[]{:S(2)}) async-start(bf16[64,2,16,128]{3,2,1,0:T(8,128)(2,1)} %get-tuple-element.18), calls=%async_computation.2 | async-start | bytes 1048576 | tf_op jit(solution)/shard_map/all_to_all | solution.py:190
where the time goes:
time: 116 us; the launch traced here: 115 us
  blocking collectives  49.7 us (43%)
  waiting for transfers between devices  28.6 us (25%)
  starting transfers between devices  23.9 us (21%)
  Pallas kernels  8.28 us (7%)
  local copies, waits for them, and re-layouts  3.36 us (3%)
    all_to_all x1, blocking collectives, shards(): docs = lax.all_to_all(picked, 'tp', 0, 0, tiled=True)  31.9 us
    all_to_all x1, blocking collectives, shards(): parts = lax.all_to_all(by_doc, 'wide', 0, 0, tiled=True)  17.8 us
    all_to_all x1, starting transfers between devices, shards(): lax.all_to_all(jnp.broadcast_to(slab, (wide_width,) + slab.shape[1:]), 'w...  17.5 us
    all_to_all x1, waiting for transfers between devices, shards(): back = lax.all_to_all(d_docs, 'tp', 0, 0, tiled=True)  16.9 us
    all_to_all x1, waiting for transfers between devices, shards(): lax.all_to_all(jnp.broadcast_to(slab, (wide_width,) + slab.shape[1:]), 'w...  11.8 us
    pallas_call x1, Pallas kernels, attention(): pl.pallas_call(functools.partial(attention_kernel, heads, uses), out_shap...  7.74 us
    all_to_all x1, starting transfers between devices, shards(): back = lax.all_to_all(d_docs, 'tp', 0, 0, tiled=True)  6.42 us
  transfers between devices with their start and end apart: 2, of which 2 were waited for; matrix products, arithmetic and copies ran while one was open for 0% of the time, Pallas kernels for 0%

commit v1 on v0

--- a/solution.py
+++ b/solution.py
@@ -103,12 +103,69 @@
     )(q, g, own, limits, docs)
 
 
-def select_kernel(reads_ref, every_ref, out_ref, rows_ref):
+def row_of(kind, doc, token, head, docs_here, block_len):
+    return ((head * 2 + kind) * docs_here + doc) * block_len + token
+
+
+def slab_kernel(doc_ref, out_ref):
+    copies, per_owner, head_dim = out_ref.shape
+    lines = doc_ref[...].reshape(-1, doc_ref.shape[3])
+    heads = lines.shape[1] // head_dim
+    slab = jnp.concatenate(
+        [lines[:, h * head_dim : (h + 1) * head_dim] for h in range(heads)], axis=0
+    )
+    for i in range(copies):
+        out_ref[i] = slab
+
+
+def total_kernel(parts_ref, out_ref):
+    owners, per_owner, head_dim = parts_ref.shape
+    total = parts_ref[0].astype(jnp.float32)
+    for i in range(1, owners):
+        total = total + parts_ref[i].astype(jnp.float32)
+    heads = out_ref.shape[3] // head_dim
+    lines = per_owner // heads
+    whole = jnp.concatenate(
+        [total[h * lines : (h + 1) * lines] for h in range(heads)], axis=1
+    )
+    out_ref[...] = whole.reshape(out_ref.shape)
+
+
+def select_kernel(ids_ref, lengths_ref, every_ref, out_ref, reads_ref, limit_ref, rows_ref):
     owners, per_owner, head_dim = every_ref.shape
     subs, kv_heads, _, per_piece, _ = out_ref.shape
-    docs_here = reads_ref.shape[1] // owners
-    block_len = per_owner // (2 * docs_here * kv_heads)
-    uses = per_piece // block_len
+    uses, rollouts = ids_ref.shape
+    docs = lengths_ref.shape[1]
+    docs_here = docs // owners
+    block_len = per_piece // uses
+    group = lax.axis_index("wide")
+    my_sub = lax.axis_index("tp") // kv_heads
+
+    ids = ids_ref[...].astype(jnp.float32)
+    place = lax.broadcasted_iota(jnp.int32, (uses, rollouts), 1)
+
+    def documents(sub):
+        mine = place == group * subs + sub
+        return jnp.sum(jnp.where(mine, ids, 0.0), axis=1, keepdims=True).astype(jnp.int32)
+
+    column = lax.broadcasted_iota(jnp.int32, (uses, docs), 1)
+    named = column % owners * docs_here + column // owners
+    reads = jnp.concatenate(
+        [(documents(sub) == named).astype(jnp.float32) for sub in range(subs)], axis=0
+    ).astype(jnp.bfloat16)
+    reads_ref[...] = reads
+
+    lengths = lengths_ref[...].astype(jnp.float32)
+    my_lengths = jnp.sum(
+        jnp.where(documents(my_sub) == column, lengths, 0.0), axis=1, keepdims=True
+    )
+    wide_row = (uses, 128)
+    use = lax.broadcasted_iota(jnp.int32, wide_row, 0)
+    lane = lax.broadcasted_iota(jnp.int32, wide_row, 1)
+    limits = jnp.sum(jnp.where(lane % uses == use, my_lengths, 0.0), axis=0, keepdims=True)
+    limits = limits.astype(jnp.int32)
+    limit_ref[...] = jnp.concatenate([limits] * (limit_ref.shape[1] // 128), axis=1)
+
     rows_ref[...] = every_ref[...].astype(jnp.float32).reshape(owners * per_owner, head_dim)
     for kind in range(2):
         found = []
@@ -116,12 +173,12 @@
             columns = []
             for h in range(kv_heads):
                 of_head = [
-                    rows_ref[pl.ds(((kind * docs_here + doc) * block_len + token) * kv_heads + h, owners, stride=per_owner), :]
+                    rows_ref[pl.ds(row_of(kind, doc, token, h, docs_here, block_len), owners, stride=per_owner), :]
                     for doc in range(docs_here)
                 ]
                 columns.append(jnp.concatenate(of_head, axis=0))
             table = jnp.concatenate(columns, axis=1).astype(jnp.bfloat16)
-            found.append(dot(reads_ref[...], table, NN))
+            found.append(dot(reads, table, NN))
         for h in range(kv_heads):
             piece = [
                 part[:, h * head_dim : (h + 1) * head_dim].reshape(subs, uses, head_dim)
@@ -130,75 +187,84 @@
             out_ref[:, h, kind] = jnp.concatenate(piece, axis=1).astype(jnp.bfloat16)
 
 
-def select(reads, every, subs, kv_heads, per_piece):
-    owners, per_owner, head_dim = every.shape
+def combine_kernel(reads_ref, back_ref, out_ref, rows_ref):
+    owners, per_owner, head_dim = out_ref.shape
+    subs, kv_heads, _, per_piece, _ = back_ref.shape
+    docs_here = reads_ref.shape[1] // owners
+    uses = reads_ref.shape[0] // subs
+    block_len = per_piece // uses
+    reads = reads_ref[...]
+    for kind in range(2):
+        pieces = [back_ref[:, h, kind].astype(jnp.float32) for h in range(kv_heads)]
+        for token in range(block_len):
+            table = jnp.concatenate(
+                [
+                    piece[:, token * uses : (token + 1) * uses].reshape(subs * uses, head_dim)
+                    for piece in pieces
+                ],
+                axis=1,
+            ).astype(jnp.bfloat16)
+            sums = dot(reads, table, TN)
+            for h in range(kv_heads):
+                for doc in range(docs_here):
+                    row = row_of(kind, doc, token, h, docs_here, block_len)
+                    rows_ref[pl.ds(row, owners, stride=per_owner), :] = sums[
+                        doc * owners : (doc + 1) * owners, h * head_dim : (h + 1) * head_dim
+                    ]
+    out_ref[...] = rows_ref[...].astype(jnp.bfloat16).reshape(out_ref.shape)
+
+
+def local(kernel, out, *args, scratch=(), flops=0):
     vmem = pl.BlockSpec(memory_space=pltpu.VMEM)
+    many = isinstance(out, tuple)
+    size = sum(x.size * x.dtype.itemsize for x in args)
     return pl.pallas_call(
-        select_kernel,
-        out_shape=jax.ShapeDtypeStruct((subs, kv_heads, 2, per_piece, head_dim), jnp.bfloat16),
-        in_specs=[vmem] * 2,
-        out_specs=vmem,
-        scratch_shapes=[pltpu.VMEM((owners * per_owner, head_dim), jnp.float32)],
+        kernel,
+        out_shape=out,
+        in_specs=[vmem] * len(args),
+        out_specs=(vmem,) * len(out) if many else vmem,
+        scratch_shapes=list(scratch),
         compiler_params=pltpu.CompilerParams(vmem_limit_bytes=16 * 1024 * 1024),
-        cost_estimate=pl.CostEstimate(
-            flops=2 * reads.size * per_owner * head_dim,
-            bytes_accessed=6 * every.size,
-            transcendentals=0,
-        ),
-    )(reads, every)
+        cost_estimate=pl.CostEstimate(flops=flops, bytes_accessed=2 * size, transcendentals=0),
+    )(*args)
 
 
 def shards(queries, own_kv, doc_kv, doc_lengths, doc_ids, d_out):
     tp_width = lax.axis_size("tp")
     wide_width = lax.axis_size("wide")
-    my_group = lax.axis_index("wide")
     head_dim = own_kv.shape[4]
     kv_heads = doc_kv.shape[3] // head_dim
     subs = tp_width // kv_heads
-    my_sub = lax.axis_index("tp") // kv_heads
     docs_here, block_len = doc_kv.shape[1:3]
     uses = doc_ids.shape[1]
     slots = tp_width * block_len * uses
-
-    slab = doc_kv.reshape(1, -1, head_dim)
-    every = lax.all_to_all(
-        jnp.broadcast_to(slab, (wide_width,) + slab.shape[1:]), "wide", 0, 0, tiled=True
-    )
-    doc_ids, doc_lengths, every = lax.optimization_barrier((doc_ids, doc_lengths, every))
-
-    by_sub = lax.dynamic_index_in_dim(
-        doc_ids.reshape(wide_width, subs, uses), my_group, 0, keepdims=False
-    )
-    order = jnp.arange(wide_width * docs_here, dtype=jnp.int32)
-    order = order.reshape(wide_width, docs_here).T.reshape(-1)
-    reads = (by_sub[:, :, None] == order).astype(jnp.bfloat16).reshape(subs * uses, -1)
-    chosen = lax.dynamic_index_in_dim(by_sub, my_sub, 0, keepdims=False)
-    lengths = jnp.sum(
-        jnp.where(chosen[:, None] == jnp.arange(doc_lengths.shape[0], dtype=jnp.int32), doc_lengths, 0), axis=1
-    )
-    limits = jnp.tile(lengths, slots // uses)[None]
-
-    picked = select(reads, every, subs, kv_heads, block_len * uses)
-    picked = picked.reshape(tp_width, 2, block_len * uses, head_dim)
-    picked, limits = lax.optimization_barrier((picked, limits))
-    docs = lax.all_to_all(picked, "tp", 0, 0, tiled=True)
+    low = jnp.bfloat16
+    per_owner = 2 * docs_here * block_len * kv_heads
+    per_piece = block_len * uses
+
+    slabs = jax.ShapeDtypeStruct((wide_width, per_owner, head_dim), low)
+    pieces = jax.ShapeDtypeStruct((subs, kv_heads, 2, per_piece, head_dim), low)
+    reads = jax.ShapeDtypeStruct((subs * uses, wide_width * docs_here), low)
+    limits = jax.ShapeDtypeStruct((1, slots), jnp.int32)
+    rows = pltpu.VMEM((wide_width * per_owner, head_dim), jnp.float32)
+    flops = 2 * subs * uses * wide_width * docs_here * per_owner // docs_here * head_dim
+
+    every = lax.all_to_all(local(slab_kernel, slabs, doc_kv), "wide", 0, 0, tiled=True)
+    picked, reads, limits = local(
+        select_kernel, (pieces, reads, limits), doc_ids.T, doc_lengths[None], every, scratch=(rows,), flops=flops
+    )
+    docs = lax.all_to_all(
+        picked.reshape(tp_width, 2, per_piece, head_dim), "tp", 0, 0, tiled=True
+    )
 
     attended, d_query, d_docs = attention(
         queries[0, 0], d_out[0, 0], own_kv[:, 0, 0], limits, docs, uses
     )
 
-    back = lax.all_to_all(d_docs, "tp", 0, 0, tiled=True)
-    back = back.reshape(subs, kv_heads, 2, block_len, uses, head_dim)
-    by_doc = jnp.einsum(
-        "zudw,zhktul->wkdthl",
-        reads.reshape(subs, uses, docs_here, wide_width),
-        back,
-        preferred_element_type=jnp.float32,
-    ).astype(jnp.bfloat16)
-    by_doc = by_doc.reshape(wide_width, -1, head_dim)
+    back = lax.all_to_all(d_docs, "tp", 0, 0, tiled=True).reshape(pieces.shape)
+    by_doc = local(combine_kernel, slabs, reads, back, scratch=(rows,), flops=flops)
     parts = lax.all_to_all(by_doc, "wide", 0, 0, tiled=True)
-    d_doc = jnp.sum(parts.astype(jnp.float32), axis=0)
-    d_doc = d_doc.reshape(2, docs_here, block_len, kv_heads * head_dim)
+    d_doc = local(total_kernel, jax.ShapeDtypeStruct(doc_kv.shape, jnp.float32), parts)
     return attended[None, None], d_query[None, None], d_doc
 
 

time: 116 us -> 114 us (0.983)
  blocking collectives: 49.7 us -> 102 us
  waiting for transfers between devices: 28.6 us -> 0 us
  starting transfers between devices: 23.9 us -> 0 us
  local copies, waits for them, and re-layouts: 3.36 us -> 1.39 us
    all_to_all x1 -> x3, blocking collectives: 31.9 us -> 84.1 us  [the longest x1 32.6 us: shards(): lax.all_to_all(picked.reshape(tp_width, 2, per_piece, head_dim), 'tp', 0,...]
    all_to_all x2 -> x0, waiting for transfers between devices: 28.6 us -> none  [the longest x1 16.9 us: shards(): back = lax.all_to_all(d_docs, 'tp', 0, 0, tiled=True)]
    all_to_all x2 -> x0, starting transfers between devices: 23.9 us -> none  [the longest x1 17.5 us: shards(): lax.all_to_all(jnp.broadcast_to(slab, (wide_width,) + slab.shape[1:]), 'w...]
    broadcast_in_dim x2 -> x0, local copies, waits for them, and re-layouts: 1.49 us -> none  [shards(): jnp.broadcast_to(slab, (wide_width,) + slab.shape[1:])]
    pallas_call x1 -> x4, Pallas kernels: 0.54 us -> 1.75 us  [local(): pl.pallas_call(kernel, out_shape=out, in_specs=[vmem] * len(args), out_sp...]
  transfers between devices with their start and end apart: 2 -> 0, of which waited for: 2 -> 0; matrix products, arithmetic and copies ran while one was open for 0% -> 0% of each run, Pallas kernels for 0% -> 0%
where the time goes in v1:
time: 114 us; the launch traced here: 113 us
  blocking collectives  102 us (89%)
  Pallas kernels  9.31 us (8%)
  local copies, waits for them, and re-layouts  1.39 us (1%)
    all_to_all x1, blocking collectives, shards(): lax.all_to_all(picked.reshape(tp_width, 2, per_piece, head_dim), 'tp', 0,...  32.6 us
    all_to_all x1, blocking collectives, shards(): lax.all_to_all(local(slab_kernel, slabs, doc_kv), 'wide', 0, 0, tiled=True)  28.4 us
    all_to_all x1, blocking collectives, shards(): back = lax.all_to_all(d_docs, 'tp', 0, 0, tiled=True).reshape(pieces.shape)  23.1 us
    all_to_all x1, blocking collectives, shards(): parts = lax.all_to_all(by_doc, 'wide', 0, 0, tiled=True)  17.9 us
    pallas_call x1, Pallas kernels, attention(): pl.pallas_call(functools.partial(attention_kernel, heads, uses), out_shap...  7.56 us

profile of v1, /device:TPU:1, one launch (start us, length us, event | category | flops | bytes accessed | tf_op | source)
XLA Modules:
  0.0 113.4 jit_solution(14823891556222118659)
XLA Ops:
  0.6 0.0 copy-start
  0.6 0.7 copy-done
  1.3 0.1 shard_map.85
  1.4 0.0 copy-start.1
  1.4 28.4 %all_to_all.20.every_ref = bf16[16,64,128]{2,1,0:T(8,128)(2,1)S(1)} all-to-all(bf16[16,64,128]{2,1,0:T(8,128)(2,1)S(1)} %shard_map.85), channel_id=1, replica_groups=mesh['wide'=16,'tp'=64] {'wide'}, dimensions={0} | all-to-all | bytes 524288 | tf_op jit(solution)/shard_map/all_to_all | solution.py:252
  29.8 0.0 copy-start.2
  29.9 0.0 copy-done.1
  29.9 0.7 copy-done.2
  30.5 0.5 shard_map.86
  31.1 0.0 copy-start.3
  31.1 0.0 copy-start.4
  31.1 0.0 copy-start.5
  31.1 32.6 %all_to_all.21.doc_ref = bf16[64,2,16,128]{3,2,1,0:T(8,128)(2,1)S(1)} all-to-all(bf16[64,2,16,128]{3,2,1,0:T(8,128)(2,1)S(1)} %bitcast.10), channel_id=1, replica_groups=mesh['wide'=16,'tp'=64] {'tp'}, dimensions={0} | all-to-all | bytes 1048576 | tf_op jit(solution)/shard_map/all_to_all | solution.py:256
  63.7 0.0 copy-done.3
  63.7 0.0 copy-done.4
  63.7 0.0 copy-done.5
  63.7 7.6 %shard_map.87 = (bf16[192,1024]{1,0:T(8,128)(2,1)}, bf16[192,1024]{1,0:T(8,128)(2,1)}, bf16[64,2,16,128]{3,2,1,0:T(8,128)(2,1)S(1)}) custom-call(bf16[192,1024]{1,0:T(8,128)(2,1)S(1)} %bitcast.13, bf16[192,1024]{1,0:T(8,128)(2,1)S(1)} %bitcast.14, bf16[2,192,128]{2,1,0:T(8,128)(2,1)S(1)} %bitcast.15, s32[1,1024]{1,0:T(1,128)S(1)} %get-tuple-element.9.limit_ref, ...), custom_call_target="tpu_custom_call" | custom-call | flops 2868903936 | bytes 2621440 | tf_op jit(solution)/shard_map/pallas_call | solution.py:87
  71.2 23.1 %all_to_all.22 = bf16[64,2,16,128]{3,2,1,0:T(8,128)(2,1)S(1)} all-to-all(bf16[64,2,16,128]{3,2,1,0:T(8,128)(2,1)S(1)} %get-tuple-element.14), channel_id=1, replica_groups=mesh['wide'=16,'tp'=64] {'tp'}, dimensions={0} | all-to-all | bytes 1048576 | tf_op jit(solution)/shard_map/all_to_all | solution.py:264
  94.3 0.5 shard_map.88
  94.8 17.9 %all_to_all.23.parts_ref = bf16[16,64,128]{2,1,0:T(8,128)(2,1)S(1)} all-to-all(bf16[16,64,128]{2,1,0:T(8,128)(2,1)S(1)} %shard_map.88), channel_id=1, replica_groups=mesh['wide'=16,'tp'=64] {'wide'}, dimensions={0} | all-to-all | bytes 524288 | tf_op jit(solution)/shard_map/all_to_all | solution.py:266
  112.7 0.7 shard_map.89
Async XLA Ops:
  0.6 0.7 copy-start
  1.4 28.4 %copy-start.1 = (s32[128,8]{0,1:T(8,128)S(1)}, s32[128,8]{0,1:T(8,128)}, u32[]{:S(2)}) copy-start(s32[128,8]{0,1:T(8,128)} %param.10) | copy-start | bytes 12292
  29.8 0.7 copy-start.2
  31.1 32.6 %copy-start.3 = (bf16[1,1,192,1024]{3,2,1,0:T(8,128)(2,1)S(1)}, bf16[1,1,192,1024]{3,2,1,0:T(8,128)(2,1)}, u32[]{:S(2)}) copy-start(bf16[1,1,192,1024]{3,2,1,0:T(8,128)(2,1)} %param.6) | copy-start | bytes 1179652
  31.1 32.6 %copy-start.4 = (bf16[1,1,192,1024]{3,2,1,0:T(8,128)(2,1)S(1)}, bf16[1,1,192,1024]{3,2,1,0:T(8,128)(2,1)}, u32[]{:S(2)}) copy-start(bf16[1,1,192,1024]{3,2,1,0:T(8,128)(2,1)} %param.11) | copy-start | bytes 1179652
  31.1 32.6 %copy-start.5 = (bf16[2,1,1,192,128]{4,3,2,1,0:T(8,128)(2,1)S(1)}, bf16[2,1,1,192,128]{4,3,2,1,0:T(8,128)(2,1)}, u32[]{:S(2)}) copy-start(bf16[2,1,1,192,128]{4,3,2,1,0:T(8,128)(2,1)} %param.7) | copy-start | bytes 294916

commit v2 on v1

v2 whole, which is shorter than its diff:
```python
import functools
import math

import jax
import jax.numpy as jnp
from jax import lax
from jax.experimental import pallas as pl
from jax.experimental.pallas import tpu as pltpu
from jax.sharding import PartitionSpec as P

NT = (((1,), (1,)), ((), ()))
NN = (((1,), (0,)), ((), ()))
TN = (((0,), (0,)), ((), ()))
OUT_OF_REACH = -2e38
STACK = 4
VMEM_BYTES = 48 * 1024 * 1024


def dot(a, b, dims):
    return lax.dot_general(a, b, dims, preferred_element_type=jnp.float32)


def documents(ids_ref, subs, sub):
    uses, rollouts = ids_ref.shape
    place = lax.broadcasted_iota(jnp.int32, (uses, rollouts), 1)
    mine = place == lax.axis_index("wide") * subs + sub
    ids = jnp.where(mine, ids_ref[...].astype(jnp.float32), 0.0)
    return jnp.sum(ids, axis=1, keepdims=True).astype(jnp.int32)


def length_row(subs, kv_heads, slots, ids_ref, lengths_ref):
    mine = documents(ids_ref, subs, lax.axis_index("tp") // kv_heads)
    uses, docs = ids_ref.shape[0], lengths_ref.shape[1]
    column = lax.broadcasted_iota(jnp.int32, (uses, docs), 1)
    lengths = jnp.where(mine == column, lengths_ref[...].astype(jnp.float32), 0.0)
    lengths = jnp.sum(lengths, axis=1, keepdims=True)
    use = lax.broadcasted_iota(jnp.int32, (uses, 128), 0)
    lane = lax.broadcasted_iota(jnp.int32, (uses, 128), 1)
    row = jnp.sum(jnp.where(lane % uses == use, lengths, 0.0), axis=0, keepdims=True)
    return jnp.concatenate([row.astype(jnp.int32)] * (slots // 128), axis=1)


class Rollout:
    def __init__(self, uses, q_ref, g_ref, own_ref, doc_ref, limits):
        self.q_ref, self.g_ref = q_ref, g_ref
        sources, _, per_source, self.head_dim = doc_ref.shape
        self.rows = q_ref.shape[0]
        self.heads = q_ref.shape[1] // self.head_dim
        slots = sources * per_source
        self.scale = 1.0 / math.sqrt(self.head_dim)
        self.doc_k = doc_ref[:, 0].reshape(slots, self.head_dim)
        self.doc_v = doc_ref[:, 1].reshape(slots, self.head_dim)
        self.own_k, self.own_v = own_ref[0], own_ref[1]
        token = lax.broadcasted_iota(jnp.int32, (1, slots), 1) // uses
        self.doc_allowed = token < limits
        square = (self.rows, self.rows)
        causal = lax.broadcasted_iota(jnp.int32, square, 1) <= lax.broadcasted_iota(
            jnp.int32, square, 0
        )
        self.causal = jnp.concatenate([causal.astype(jnp.int32)] * STACK, axis=0) > 0

    def stacked(self, ref, first):
        return jnp.concatenate(
            [
                ref[:, pl.ds((first + h) * self.head_dim, self.head_dim)]
                for h in range(STACK)
            ],
            axis=0,
        )

    def unstack(self, ref, first, value):
        for h in range(STACK):
            ref[:, pl.ds((first + h) * self.head_dim, self.head_dim)] = value[
                h * self.rows : (h + 1) * self.rows
            ]

    def heads_from(self, first):
        low = jnp.bfloat16
        exponent = self.scale * math.log2(math.e)
        q, g = self.stacked(self.q_ref, first), self.stacked(self.g_ref, first)
        s_doc = jnp.where(self.doc_allowed, dot(q, self.doc_k, NT), OUT_OF_REACH)
        s_own = jnp.where(self.causal, dot(q, self.own_k, NT), OUT_OF_REACH)
        top = jnp.maximum(
            jnp.max(s_doc, axis=1, keepdims=True), jnp.max(s_own, axis=1, keepdims=True)
        )
        e_doc = jnp.exp2((s_doc - top) * exponent)
        e_own = jnp.exp2((s_own - top) * exponent)
        total = jnp.sum(e_doc, axis=1, keepdims=True) + jnp.sum(e_own, axis=1, keepdims=True)
        inverse = 1.0 / total
        w_doc, w_own = e_doc * inverse, e_own * inverse
        w_doc_low, w_own_low = w_doc.astype(low), w_own.astype(low)
        att = (dot(w_doc_low, self.doc_v, NN) + dot(w_own_low, self.own_v, NN)).astype(low)
        row_dot = jnp.sum(
            g.astype(jnp.float32) * att.astype(jnp.float32), axis=1, keepdims=True
        )
        ds_doc = (w_doc * (dot(g, self.doc_v, NT) - row_dot)).astype(low)

        def ds_own():
            return (w_own * (dot(g, self.own_v, NT) - row_dot)).astype(low)

        return q, g, w_doc_low, att, ds_doc, ds_own


def document_kernel(
    subs, kv_heads, q_ref, g_ref, own_ref, ids_ref, lengths_ref, doc_ref, dkv_ref, limit_ref, dk_sum, dv_sum
):
    low = jnp.bfloat16
    sources, _, per_source, head_dim = doc_ref.shape
    limits = length_row(subs, kv_heads, sources * per_source, ids_ref, lengths_ref)
    limit_ref[...] = limits
    rollout = Rollout(ids_ref.shape[0], q_ref, g_ref, own_ref, doc_ref, limits)
    for first in range(0, rollout.heads, STACK):
        q, g, w_doc, _, ds_doc, _ = rollout.heads_from(first)
        dk, dv = dot(q.T, ds_doc, NN), dot(g.T, w_doc, NN)
        if first:
            dk, dv = dk_sum[...] + dk, dv_sum[...] + dv
        if first + STACK < rollout.heads:
            dk_sum[...] = dk
            dv_sum[...] = dv
        else:
            dk = dk.T * rollout.scale
            dkv_ref[:, 0] = dk.astype(low).reshape(sources, per_source, head_dim)
            dkv_ref[:, 1] = dv.T.astype(low).reshape(sources, per_source, head_dim)


def query_kernel(uses, q_ref, g_ref, own_ref, limit_ref, doc_ref, att_ref, dq_ref, ready_ref):
    ready_ref[...] = limit_ref[...]
    rollout = Rollout(uses, q_ref, g_ref, own_ref, doc_ref, limit_ref[...])
    for first in range(0, rollout.heads, STACK):
        _, _, _, att, ds_doc, ds_own = rollout.heads_from(first)
        dq = dot(ds_doc, rollout.doc_k, NN) + dot(ds_own(), rollout.own_k, NN)
        rollout.unstack(att_ref, first, att)
        rollout.unstack(dq_ref, first, (dq * rollout.scale).astype(jnp.bfloat16))


def attention(q, g, own, ids, lengths, docs, subs, kv_heads):
    rows, width = q.shape
    head_dim = own.shape[2]
    slots = docs.size // (2 * head_dim)
    uses = ids.shape[0]
    vmem = pl.BlockSpec(memory_space=pltpu.VMEM)
    pairs = width // head_dim * rows * (slots + rows)

    def call(kernel, out, *args, scratch=()):
        return pl.pallas_call(
            kernel,
            out_shape=out,
            in_specs=[vmem] * len(args),
            out_specs=(vmem,) * len(out),
            scratch_shapes=list(scratch),
            compiler_params=pltpu.CompilerParams(vmem_limit_bytes=VMEM_BYTES),
            cost_estimate=pl.CostEstimate(
                flops=10 * pairs * head_dim,
                bytes_accessed=2 * (2 * q.size + 2 * docs.size),
                transcendentals=pairs,
            ),
        )(*args)

    d_docs, limits = call(
        functools.partial(document_kernel, subs, kv_heads),
        (
            jax.ShapeDtypeStruct(docs.shape, jnp.bfloat16),
            jax.ShapeDtypeStruct((1, slots), jnp.int32),
        ),
        q, g, own, ids, lengths, docs,
        scratch=[pltpu.VMEM((head_dim, slots), jnp.float32)] * 2,
    )
    attended, d_query, ready = call(
        functools.partial(query_kernel, uses),
        (jax.ShapeDtypeStruct(q.shape, jnp.bfloat16),) * 2
        + (jax.ShapeDtypeStruct(limits.shape, limits.dtype),),
        q, g, own, limits, docs,
    )
    return attended, d_query, ready, d_docs


def row_of(kind, doc, token, head, docs_here, block_len):
    return ((head * 2 + kind) * docs_here + doc) * block_len + token


def slab_kernel(doc_ref, out_ref):
    copies, per_owner, head_dim = out_ref.shape
    lines = doc_ref[...].reshape(-1, doc_ref.shape[3])
    heads = lines.shape[1] // head_dim
    slab = jnp.concatenate(
        [lines[:, h * head_dim : (h + 1) * head_dim] for h in range(heads)], axis=0
    )
    for i in range(copies):
        out_ref[i] = slab


def total_kernel(parts_ref, out_ref):
    owners, per_owner, head_dim = parts_ref.shape
    total = parts_ref[0].astype(jnp.float32)
    for i in range(1, owners):
        total = total + parts_ref[i].astype(jnp.float32)
    heads = out_ref.shape[3] // head_dim
    lines = per_owner // heads
    whole = jnp.concatenate(
        [total[h * lines : (h + 1) * lines] for h in range(heads)], axis=1
    )
    out_ref[...] = whole.reshape(out_ref.shape)


def select_kernel(ids_ref, every_ref, out_ref, reads_ref, rows_ref):
    owners, per_owner, head_dim = every_ref.shape
    subs, kv_heads, _, per_piece, _ = out_ref.shape
    uses = ids_ref.shape[0]
    docs = reads_ref.shape[1]
    docs_here = docs // owners
    block_len = per_piece // uses
    column = lax.broadcasted_iota(jnp.int32, (uses, docs), 1)
    named = column % owners * docs_here + column // owners
    reads = jnp.concatenate(
        [
            (documents(ids_ref, subs, sub) == named).astype(jnp.float32)
            for sub in range(subs)
        ],
        axis=0,
    ).astype(jnp.bfloat16)
    reads_ref[...] = reads
    rows_ref[...] = every_ref[...].astype(jnp.float32).reshape(owners * per_owner, head_dim)
    for kind in range(2):
        found = []
        for token in range(block_len):
            columns = []
            for h in range(kv_heads):
                of_head = [
                    rows_ref[pl.ds(row_of(kind, doc, token, h, docs_here, block_len), owners, stride=per_owner), :]
                    for doc in range(docs_here)
                ]
                columns.append(jnp.concatenate(of_head, axis=0))
            table = jnp.concatenate(columns, axis=1).astype(jnp.bfloat16)
            found.append(dot(reads, table, NN))
        for h in range(kv_heads):
            piece = [
                part[:, h * head_dim : (h + 1) * head_dim].reshape(subs, uses, head_dim)
                for part in found
            ]
            out_ref[:, h, kind] = jnp.concatenate(piece, axis=1).astype(jnp.bfloat16)


def combine_kernel(ready_ref, reads_ref, back_ref, out_ref, rows_ref):
    owners, per_owner, head_dim = out_ref.shape
    subs, kv_heads, _, per_piece, _ = back_ref.shape
    docs_here = reads_ref.shape[1] // owners
    uses = reads_ref.shape[0] // subs
    block_len = per_piece // uses
    reads = reads_ref[...]
    for kind in range(2):
        pieces = [back_ref[:, h, kind].astype(jnp.float32) for h in range(kv_heads)]
        for token in range(block_len):
            table = jnp.concatenate(
                [
                    piece[:, token * uses : (token + 1) * uses].reshape(subs * uses, head_dim)
                    for piece in pieces
                ],
                axis=1,
            ).astype(jnp.bfloat16)
            sums = dot(reads, table, TN)
            for h in range(kv_heads):
                for doc in range(docs_here):
                    row = row_of(kind, doc, token, h, docs_here, block_len)
                    rows_ref[pl.ds(row, owners, stride=per_owner), :] = sums[
                        doc * owners : (doc + 1) * owners, h * head_dim : (h + 1) * head_dim
                    ]
    out_ref[...] = rows_ref[...].astype(jnp.bfloat16).reshape(out_ref.shape)


def local(kernel, out, *args, scratch=(), flops=0):
    vmem = pl.BlockSpec(memory_space=pltpu.VMEM)
    many = isinstance(out, tuple)
    size = sum(x.size * x.dtype.itemsize for x in args)
    return pl.pallas_call(
        kernel,
        out_shape=out,
        in_specs=[vmem] * len(args),
        out_specs=(vmem,) * len(out) if many else vmem,
        scratch_shapes=list(scratch),
        compiler_params=pltpu.CompilerParams(vmem_limit_bytes=16 * 1024 * 1024),
        cost_estimate=pl.CostEstimate(flops=flops, bytes_accessed=2 * size, transcendentals=0),
    )(*args)


def shards(queries, own_kv, doc_kv, doc_lengths, doc_ids, d_out):
    tp_width = lax.axis_size("tp")
    wide_width = lax.axis_size("wide")
    head_dim = own_kv.shape[4]
    kv_heads = doc_kv.shape[3] // head_dim
    subs = tp_width // kv_heads
    docs_here, block_len = doc_kv.shape[1:3]
    uses = doc_ids.shape[1]
    low = jnp.bfloat16
    per_owner = 2 * docs_here * block_len * kv_heads
    per_piece = block_len * uses

    slabs = jax.ShapeDtypeStruct((wide_width, per_owner, head_dim), low)
    pieces = jax.ShapeDtypeStruct((subs, kv_heads, 2, per_piece, head_dim), low)
    reads = jax.ShapeDtypeStruct((subs * uses, wide_width * docs_here), low)
    ids = doc_ids.T
    rows = pltpu.VMEM((wide_width * per_owner, head_dim), jnp.float32)
    flops = 2 * subs * uses * wide_width * docs_here * per_owner // docs_here * head_dim

    every = lax.all_to_all(local(slab_kernel, slabs, doc_kv), "wide", 0, 0, tiled=True)
    picked, reads = local(
        select_kernel, (pieces, reads), ids, every, scratch=(rows,), flops=flops
    )
    docs = lax.all_to_all(
        picked.reshape(tp_width, 2, per_piece, head_dim), "tp", 0, 0, tiled=True
    )

    attended, d_query, ready, d_docs = attention(
        queries[0, 0], d_out[0, 0], own_kv[:, 0, 0], ids, doc_lengths[None], docs, subs, kv_heads
    )

    back = lax.all_to_all(d_docs, "tp", 0, 0, tiled=True).reshape(pieces.shape)
    by_doc = local(combine_kernel, slabs, ready, reads, back, scratch=(rows,), flops=flops)
    parts = lax.all_to_all(by_doc, "wide", 0, 0, tiled=True)
    d_doc = local(total_kernel, jax.ShapeDtypeStruct(doc_kv.shape, jnp.float32), parts)
    return attended[None, None], d_query[None, None], d_doc


def solution(mesh):
    placed = (
        P("wide", "tp", None, None),
        P(None, "wide", "tp", None, None),
        P(None, "wide", "tp", None),
        P(),
        P(),
        P("wide", "tp", None, None),
    )
    return jax.shard_map(
        shards,
        mesh=mesh,
        in_specs=placed,
        out_specs=(
            P("wide", "tp", None, None),
            P("wide", "tp", None, None),
            P(None, "wide", "tp", None),
        ),
        check_vma=False,
    )
```

time: 114 us -> 113 us (level)
  blocking collectives: 102 us -> 78.8 us
  waiting for transfers between devices: 0 us -> 9.64 us
  starting transfers between devices: 0 us -> 6.61 us
  Pallas kernels: 9.31 us -> 15.7 us
    all_to_all x1 -> x0, blocking collectives: 23.1 us -> none  [shards(): back = lax.all_to_all(d_docs, 'tp', 0, 0, tiled=True).reshape(pieces.shape)]
    all_to_all x0 -> x1, waiting for transfers between devices: none -> 9.64 us  [shards(): back = lax.all_to_all(d_docs, 'tp', 0, 0, tiled=True).reshape(pieces.shape)]
    all_to_all x0 -> x1, starting transfers between devices: none -> 6.61 us  [shards(): back = lax.all_to_all(d_docs, 'tp', 0, 0, tiled=True).reshape(pieces.shape)]
    pallas_call x1 -> x2, Pallas kernels: 7.56 us -> 13.9 us  [call(): pl.pallas_call(kernel, out_shape=out, in_specs=[vmem] * len(args), out_sp...]
  transfers between devices with their start and end apart: 0 -> 1, of which waited for: 0 -> 1; matrix products, arithmetic and copies ran while one was open for 0% -> 0% of each run, Pallas kernels for 0% -> 6%
where the time goes in v2:
time: 113 us
  blocking collectives  78.8 us (70%)
  Pallas kernels  15.7 us (14%)
  waiting for transfers between devices  9.64 us (9%)
  starting transfers between devices  6.61 us (6%)
  local copies, waits for them, and re-layouts  1.38 us (1%)
    all_to_all x1, blocking collectives, shards(): lax.all_to_all(picked.reshape(tp_width, 2, per_piece, head_dim), 'tp', 0,...  32.6 us
    all_to_all x1, blocking collectives, shards(): lax.all_to_all(local(slab_kernel, slabs, doc_kv), 'wide', 0, 0, tiled=True)  28.4 us
    all_to_all x1, blocking collectives, shards(): parts = lax.all_to_all(by_doc, 'wide', 0, 0, tiled=True)  17.7 us
    pallas_call x2, Pallas kernels, call(): pl.pallas_call(kernel, out_shape=out, in_specs=[vmem] * len(args), out_sp...  13.9 us
    all_to_all x1, waiting for transfers between devices, shards(): back = lax.all_to_all(d_docs, 'tp', 0, 0, tiled=True).reshape(pieces.shape)  9.64 us
    all_to_all x1, starting transfers between devices, shards(): back = lax.all_to_all(d_docs, 'tp', 0, 0, tiled=True).reshape(pieces.shape)  6.61 us
  transfers between devices with their start and end apart: 1, of which 1 were waited for; matrix products, arithmetic and copies ran while one was open for 0% of the time, Pallas kernels for 6%

profile of v2, /device:TPU:1, one launch (start us, length us, event | category | flops | bytes accessed | tf_op | source)
XLA Modules:
  0.0 112.7 jit_solution(2993588945907110379)
XLA Ops:
  0.6 0.0 copy-start
  0.6 0.7 copy-done
  1.3 0.1 shard_map.85
  1.4 0.0 copy-start.1
  1.4 28.4 %all_to_all.20.every_ref = bf16[16,64,128]{2,1,0:T(8,128)(2,1)S(1)} all-to-all(bf16[16,64,128]{2,1,0:T(8,128)(2,1)S(1)} %shard_map.85), channel_id=1, replica_groups=mesh['wide'=16,'tp'=64] {'wide'}, dimensions={0} | all-to-all | bytes 524288 | tf_op jit(solution)/shard_map/all_to_all | solution.py:304
  29.8 0.0 copy-done.1
  29.9 0.5 shard_map.86
  30.4 0.0 copy-start.2
  30.4 0.0 copy-start.3
  30.4 0.0 copy-start.4
  30.4 32.6 %all_to_all.21.doc_ref = bf16[64,2,16,128]{3,2,1,0:T(8,128)(2,1)S(1)} all-to-all(bf16[64,2,16,128]{3,2,1,0:T(8,128)(2,1)S(1)} %bitcast.10), channel_id=1, replica_groups=mesh['wide'=16,'tp'=64] {'tp'}, dimensions={0} | all-to-all | bytes 1048576 | tf_op jit(solution)/shard_map/all_to_all | solution.py:308
  63.0 0.0 copy-start.5
  63.0 0.0 copy-done.2
  63.0 0.0 copy-done.3
  63.0 0.0 copy-done.4
  63.0 0.6 copy-done.5
  63.7 6.7 %shard_map.87 = (bf16[64,2,16,128]{3,2,1,0:T(8,128)(2,1)}, s32[1,1024]{1,0:T(1,128)S(1)}) custom-call(bf16[192,1024]{1,0:T(8,128)(2,1)S(1)} %bitcast.13, bf16[192,1024]{1,0:T(8,128)(2,1)S(1)} %bitcast.15, bf16[2,192,128]{2,1,0:T(8,128)(2,1)S(1)} %bitcast.17, s32[8,128]{1,0:T(8,128)S(1)} %bitcast.12, s32[1,32]{1,0:T(1,128)S(1)} %bitcast.19, ...), custom_call_target="tpu_custom_call" | custom-call | flops 2390753280 | bytes 1835008 | tf_op jit(solution)/shard_map/pallas_call | solution.py:145
  70.4 6.6 %all-to-all-start.2 = ((bf16[64,2,16,128]{3,2,1,0:T(8,128)(2,1)}), bf16[64,2,16,128]{3,2,1,0:T(8,128)(2,1)S(1)}, u32[]{:S(2)}, u32[]{:S(2)}) async-start(bf16[64,2,16,128]{3,2,1,0:T(8,128)(2,1)} %get-tuple-element.16), calls=%async_computation.2 | async-start | bytes 1048576 | tf_op jit(solution)/shard_map/all_to_all | solution.py:316
  77.0 7.2 %shard_map.88 = (bf16[192,1024]{1,0:T(8,128)(2,1)}, bf16[192,1024]{1,0:T(8,128)(2,1)}, s32[1,1024]{1,0:T(1,128)S(1)}) custom-call(bf16[192,1024]{1,0:T(8,128)(2,1)S(1)} %bitcast.14, bf16[192,1024]{1,0:T(8,128)(2,1)S(1)} %bitcast.16, bf16[2,192,128]{2,1,0:T(8,128)(2,1)S(1)} %bitcast.18, s32[1,1024]{1,0:T(1,128)S(1)} %get-tuple-element.11.limit_ref, ...), custom_call_target="tpu_custom_call" | custom-call | flops 2390753280 | bytes 1835008 | tf_op jit(solution)/shard_map/pallas_call | solution.py:145
  84.2 9.6 %all-to-all-done.2 = bf16[64,2,16,128]{3,2,1,0:T(8,128)(2,1)S(1)} async-done(((bf16[64,2,16,128]{3,2,1,0:T(8,128)(2,1)}), bf16[64,2,16,128]{3,2,1,0:T(8,128)(2,1)S(1)}, u32[]{:S(2)}, u32[]{:S(2)}) %all-to-all-start.2) | async-done | bytes 524320 | tf_op jit(solution)/shard_map/all_to_all | solution.py:316
  93.8 0.5 shard_map.89
  94.3 17.7 %all_to_all.22.parts_ref = bf16[16,64,128]{2,1,0:T(8,128)(2,1)S(1)} all-to-all(bf16[16,64,128]{2,1,0:T(8,128)(2,1)S(1)} %shard_map.89), channel_id=1, replica_groups=mesh['wide'=16,'tp'=64] {'wide'}, dimensions={0} | all-to-all | bytes 524288 | tf_op jit(solution)/shard_map/all_to_all | solution.py:318
  112.1 0.7 shard_map.90
Async XLA Ops:
  0.6 0.7 copy-start
  1.4 28.4 %copy-start.1 = (s32[128,8]{0,1:T(8,128)S(1)}, s32[128,8]{0,1:T(8,128)}, u32[]{:S(2)}) copy-start(s32[128,8]{0,1:T(8,128)} %param.10) | copy-start | bytes 12292
  30.4 32.6 %copy-start.2 = (bf16[1,1,192,1024]{3,2,1,0:T(8,128)(2,1)S(1)}, bf16[1,1,192,1024]{3,2,1,0:T(8,128)(2,1)}, u32[]{:S(2)}) copy-start(bf16[1,1,192,1024]{3,2,1,0:T(8,128)(2,1)} %param.6) | copy-start | bytes 1179652
  30.4 32.6 %copy-start.3 = (bf16[1,1,192,1024]{3,2,1,0:T(8,128)(2,1)S(1)}, bf16[1,1,192,1024]{3,2,1,0:T(8,128)(2,1)}, u32[]{:S(2)}) copy-start(bf16[1,1,192,1024]{3,2,1,0:T(8,128)(2,1)} %param.11) | copy-start | bytes 1179652
  30.4 32.6 %copy-start.4 = (bf16[2,1,1,192,128]{4,3,2,1,0:T(8,128)(2,1)S(1)}, bf16[2,1,1,192,128]{4,3,2,1,0:T(8,128)(2,1)}, u32[]{:S(2)}) copy-start(bf16[2,1,1,192,128]{4,3,2,1,0:T(8,128)(2,1)} %param.7) | copy-start | bytes 294916
  63.0 0.7 copy-start.5
  70.4 23.5 %all-to-all-start.2 = ((bf16[64,2,16,128]{3,2,1,0:T(8,128)(2,1)}), bf16[64,2,16,128]{3,2,1,0:T(8,128)(2,1)S(1)}, u32[]{:S(2)}, u32[]{:S(2)}) async-start(bf16[64,2,16,128]{3,2,1,0:T(8,128)(2,1)} %get-tuple-element.16), calls=%async_computation.2 | async-start | bytes 1048576 | tf_op jit(solution)/shard_map/all_to_all | solution.py:316

commit v3 on v2

--- a/solution.py
+++ b/solution.py
@@ -12,7 +12,8 @@
 NN = (((1,), (0,)), ((), ()))
 TN = (((0,), (0,)), ((), ()))
 OUT_OF_REACH = -2e38
-STACK = 4
+DOCUMENT_STACK = 8
+QUERY_STACK = 4
 VMEM_BYTES = 48 * 1024 * 1024
 
 
@@ -41,7 +42,8 @@
 
 
 class Rollout:
-    def __init__(self, uses, q_ref, g_ref, own_ref, doc_ref, limits):
+    def __init__(self, stack, uses, q_ref, g_ref, own_ref, doc_ref, limits):
+        self.stack = stack
         self.q_ref, self.g_ref = q_ref, g_ref
         sources, _, per_source, self.head_dim = doc_ref.shape
         self.rows = q_ref.shape[0]
@@ -57,19 +59,19 @@
         causal = lax.broadcasted_iota(jnp.int32, square, 1) <= lax.broadcasted_iota(
             jnp.int32, square, 0
         )
-        self.causal = jnp.concatenate([causal.astype(jnp.int32)] * STACK, axis=0) > 0
+        self.causal = jnp.concatenate([causal.astype(jnp.int32)] * stack, axis=0) > 0
 
     def stacked(self, ref, first):
         return jnp.concatenate(
             [
                 ref[:, pl.ds((first + h) * self.head_dim, self.head_dim)]
-                for h in range(STACK)
+                for h in range(self.stack)
             ],
             axis=0,
         )
 
     def unstack(self, ref, first, value):
-        for h in range(STACK):
+        for h in range(self.stack):
             ref[:, pl.ds((first + h) * self.head_dim, self.head_dim)] = value[
                 h * self.rows : (h + 1) * self.rows
             ]
@@ -101,20 +103,23 @@
         return q, g, w_doc_low, att, ds_doc, ds_own
 
 
+def limit_kernel(subs, kv_heads, ids_ref, lengths_ref, limit_ref):
+    limit_ref[...] = length_row(subs, kv_heads, limit_ref.shape[1], ids_ref, lengths_ref)
+
+
 def document_kernel(
-    subs, kv_heads, q_ref, g_ref, own_ref, ids_ref, lengths_ref, doc_ref, dkv_ref, limit_ref, dk_sum, dv_sum
+    uses, q_ref, g_ref, own_ref, limit_ref, doc_ref, dkv_ref, ready_ref, dk_sum, dv_sum
 ):
     low = jnp.bfloat16
     sources, _, per_source, head_dim = doc_ref.shape
-    limits = length_row(subs, kv_heads, sources * per_source, ids_ref, lengths_ref)
-    limit_ref[...] = limits
-    rollout = Rollout(ids_ref.shape[0], q_ref, g_ref, own_ref, doc_ref, limits)
-    for first in range(0, rollout.heads, STACK):
+    ready_ref[...] = limit_ref[...]
+    rollout = Rollout(DOCUMENT_STACK, uses, q_ref, g_ref, own_ref, doc_ref, limit_ref[...])
+    for first in range(0, rollout.heads, rollout.stack):
         q, g, w_doc, _, ds_doc, _ = rollout.heads_from(first)
         dk, dv = dot(q.T, ds_doc, NN), dot(g.T, w_doc, NN)
         if first:
             dk, dv = dk_sum[...] + dk, dv_sum[...] + dv
-        if first + STACK < rollout.heads:
+        if first + rollout.stack < rollout.heads:
             dk_sum[...] = dk
             dv_sum[...] = dv
         else:
@@ -125,8 +130,8 @@
 
 def query_kernel(uses, q_ref, g_ref, own_ref, limit_ref, doc_ref, att_ref, dq_ref, ready_ref):
     ready_ref[...] = limit_ref[...]
-    rollout = Rollout(uses, q_ref, g_ref, own_ref, doc_ref, limit_ref[...])
-    for first in range(0, rollout.heads, STACK):
+    rollout = Rollout(QUERY_STACK, uses, q_ref, g_ref, own_ref, doc_ref, limit_ref[...])
+    for first in range(0, rollout.heads, rollout.stack):
         _, _, _, att, ds_doc, ds_own = rollout.heads_from(first)
         dq = dot(ds_doc, rollout.doc_k, NN) + dot(ds_own(), rollout.own_k, NN)
         rollout.unstack(att_ref, first, att)
@@ -156,19 +161,17 @@
             ),
         )(*args)
 
+    row = jax.ShapeDtypeStruct((1, slots), jnp.int32)
+    limits = local(functools.partial(limit_kernel, subs, kv_heads), row, ids, lengths)
     d_docs, limits = call(
-        functools.partial(document_kernel, subs, kv_heads),
-        (
-            jax.ShapeDtypeStruct(docs.shape, jnp.bfloat16),
-            jax.ShapeDtypeStruct((1, slots), jnp.int32),
-        ),
-        q, g, own, ids, lengths, docs,
+        functools.partial(document_kernel, uses),
+        (jax.ShapeDtypeStruct(docs.shape, jnp.bfloat16), row),
+        q, g, own, limits, docs,
         scratch=[pltpu.VMEM((head_dim, slots), jnp.float32)] * 2,
     )
     attended, d_query, ready = call(
         functools.partial(query_kernel, uses),
-        (jax.ShapeDtypeStruct(q.shape, jnp.bfloat16),) * 2
-        + (jax.ShapeDtypeStruct(limits.shape, limits.dtype),),
+        (jax.ShapeDtypeStruct(q.shape, jnp.bfloat16),) * 2 + (row,),
         q, g, own, limits, docs,
     )
     return attended, d_query, ready, d_docs
@@ -202,7 +205,8 @@
     out_ref[...] = whole.reshape(out_ref.shape)
 
 
-def select_kernel(ids_ref, every_ref, out_ref, reads_ref, rows_ref):
+def select_kernel(ids_ref, every_ref, out_ref, reads_ref, ids_out_ref, rows_ref):
+    ids_out_ref[...] = ids_ref[...]
     owners, per_owner, head_dim = every_ref.shape
     subs, kv_heads, _, per_piece, _ = out_ref.shape
     uses = ids_ref.shape[0]
@@ -302,8 +306,8 @@
     flops = 2 * subs * uses * wide_width * docs_here * per_owner // docs_here * head_dim
 
     every = lax.all_to_all(local(slab_kernel, slabs, doc_kv), "wide", 0, 0, tiled=True)
-    picked, reads = local(
-        select_kernel, (pieces, reads), ids, every, scratch=(rows,), flops=flops
+    picked, reads, ids = local(
+        select_kernel, (pieces, reads, jax.ShapeDtypeStruct(ids.shape, ids.dtype)), ids, every, scratch=(rows,), flops=flops
     )
     docs = lax.all_to_all(
         picked.reshape(tp_width, 2, per_piece, head_dim), "tp", 0, 0, tiled=True

time: 113 us -> 113 us (level)
  blocking collectives: 78.8 us -> 46.3 us
  waiting for transfers between devices: 9.64 us -> 26.9 us
  starting transfers between devices: 6.61 us -> 21.2 us
    all_to_all x1 -> x0, blocking collectives: 32.6 us -> none  [shards(): lax.all_to_all(picked.reshape(tp_width, 2, per_piece, head_dim), 'tp', 0,...]
    all_to_all x0 -> x1, waiting for transfers between devices: none -> 17.4 us  [shards(): lax.all_to_all(picked.reshape(tp_width, 2, per_piece, head_dim), 'tp', 0,...]
    all_to_all x0 -> x1, starting transfers between devices: none -> 14.6 us  [shards(): lax.all_to_all(picked.reshape(tp_width, 2, per_piece, head_dim), 'tp', 0,...]
    pallas_call x4 -> x5, Pallas kernels: 1.74 us -> 2.73 us  [local(): pl.pallas_call(kernel, out_shape=out, in_specs=[vmem] * len(args), out_sp...]
  transfers between devices with their start and end apart: 1 -> 2, of which waited for: 1 -> 2; matrix products, arithmetic and copies ran while one was open for 0% -> 0% of each run, Pallas kernels for 6% -> 7%
where the time goes in v3:
time: 113 us
  blocking collectives  46.3 us (41%)
  waiting for transfers between devices  26.9 us (24%)
  starting transfers between devices  21.2 us (19%)
  Pallas kernels  16.2 us (14%)
  local copies, waits for them, and re-layouts  1.38 us (1%)
    all_to_all x1, blocking collectives, shards(): lax.all_to_all(local(slab_kernel, slabs, doc_kv), 'wide', 0, 0, tiled=True)  28.4 us
    all_to_all x1, blocking collectives, shards(): parts = lax.all_to_all(by_doc, 'wide', 0, 0, tiled=True)  17.8 us
    all_to_all x1, waiting for transfers between devices, shards(): lax.all_to_all(picked.reshape(tp_width, 2, per_piece, head_dim), 'tp', 0,...  17.4 us
    all_to_all x1, starting transfers between devices, shards(): lax.all_to_all(picked.reshape(tp_width, 2, per_piece, head_dim), 'tp', 0,...  14.6 us
    pallas_call x2, Pallas kernels, call(): pl.pallas_call(kernel, out_shape=out, in_specs=[vmem] * len(args), out_sp...  13.5 us
    all_to_all x1, waiting for transfers between devices, shards(): back = lax.all_to_all(d_docs, 'tp', 0, 0, tiled=True).reshape(pieces.shape)  9.54 us
    all_to_all x1, starting transfers between devices, shards(): back = lax.all_to_all(d_docs, 'tp', 0, 0, tiled=True).reshape(pieces.shape)  6.6 us
    pallas_call x5, Pallas kernels, local(): pl.pallas_call(kernel, out_shape=out, in_specs=[vmem] * len(args), out_sp...  2.73 us
  transfers between devices with their start and end apart: 2, of which 2 were waited for; matrix products, arithmetic and copies ran while one was open for 0% of the time, Pallas kernels for 7%

profile of v3, /device:TPU:1, one launch (start us, length us, event | category | flops | bytes accessed | tf_op | source)
XLA Modules:
  0.0 112.6 jit_solution(2893988016470391594)
XLA Ops:
  0.6 0.0 copy-start
  0.6 0.7 copy-done
  1.3 0.1 shard_map.85
  1.4 0.0 copy-start.1
  1.4 28.4 %all_to_all.20.every_ref = bf16[16,64,128]{2,1,0:T(8,128)(2,1)S(1)} all-to-all(bf16[16,64,128]{2,1,0:T(8,128)(2,1)S(1)} %shard_map.85), channel_id=1, replica_groups=mesh['wide'=16,'tp'=64] {'wide'}, dimensions={0} | all-to-all | bytes 524288 | tf_op jit(solution)/shard_map/all_to_all | solution.py:308
  29.8 0.0 copy-done.1
  29.9 1.4 %shard_map.86 = (bf16[8,8,2,16,128]{4,3,2,1,0:T(8,128)(2,1)}, bf16[64,32]{1,0:T(8,128)(2,1)S(1)}, s32[8,128]{1,0:T(8,128)S(1)}) custom-call(s32[8,128]{1,0:T(8,128)S(1)} %bitcast.10, bf16[16,64,128]{2,1,0:T(8,128)(2,1)S(1)} %all_to_all.20.every_ref), custom_call_target="tpu_custom_call" | custom-call | flops 16777216 | bytes 532480 | tf_op jit(solution)/shard_map/pallas_call | solution.py:278
  31.2 0.0 copy-start.3
  31.2 0.0 copy-start.4
  31.2 14.6 %all-to-all-start.1 = ((bf16[64,2,16,128]{3,2,1,0:T(8,128)(2,1)}), bf16[64,2,16,128]{3,2,1,0:T(8,128)(2,1)S(1)}, u32[]{:S(2)}, u32[]{:S(2)}) async-start(bf16[64,2,16,128]{3,2,1,0:T(8,128)(2,1)} %bitcast.5), calls=%async_computation.1 | async-start | bytes 1048576 | tf_op jit(solution)/shard_map/all_to_all | solution.py:312
  45.8 0.0 copy-start.2
  45.8 0.6 copy-done.2
  46.5 0.2 shard_map.87.limit_ref
  46.7 17.4 %all-to-all-done.1.doc_ref = bf16[64,2,16,128]{3,2,1,0:T(8,128)(2,1)S(1)} async-done(((bf16[64,2,16,128]{3,2,1,0:T(8,128)(2,1)}), bf16[64,2,16,128]{3,2,1,0:T(8,128)(2,1)S(1)}, u32[]{:S(2)}, u32[]{:S(2)}) %all-to-all-start.1) | async-done | bytes 524320 | tf_op jit(solution)/shard_map/all_to_all | solution.py:312
  64.0 0.0 copy-done.3
  64.0 0.0 copy-done.4
  64.0 0.0 copy-done.5
  64.0 6.3 %shard_map.88 = (bf16[64,2,16,128]{3,2,1,0:T(8,128)(2,1)}, s32[1,1024]{1,0:T(1,128)S(1)}) custom-call(bf16[192,1024]{1,0:T(8,128)(2,1)S(1)} %bitcast.12, bf16[192,1024]{1,0:T(8,128)(2,1)S(1)} %bitcast.14, bf16[2,192,128]{2,1,0:T(8,128)(2,1)S(1)} %bitcast.16, s32[1,1024]{1,0:T(1,128)S(1)} %shard_map.87.limit_ref, ...), custom_call_target="tpu_custom_call" | custom-call | flops 2390753280 | bytes 1835008 | tf_op jit(solution)/shard_map/pallas_call | solution.py:150
  70.3 6.6 %all-to-all-start.2 = ((bf16[64,2,16,128]{3,2,1,0:T(8,128)(2,1)}), bf16[64,2,16,128]{3,2,1,0:T(8,128)(2,1)S(1)}, u32[]{:S(2)}, u32[]{:S(2)}) async-start(bf16[64,2,16,128]{3,2,1,0:T(8,128)(2,1)} %get-tuple-element.18), calls=%async_computation.2 | async-start | bytes 1048576 | tf_op jit(solution)/shard_map/all_to_all | solution.py:320
  76.9 7.2 %shard_map.89 = (bf16[192,1024]{1,0:T(8,128)(2,1)}, bf16[192,1024]{1,0:T(8,128)(2,1)}, s32[1,1024]{1,0:T(1,128)S(1)}) custom-call(bf16[192,1024]{1,0:T(8,128)(2,1)S(1)} %bitcast.13, bf16[192,1024]{1,0:T(8,128)(2,1)S(1)} %bitcast.15, bf16[2,192,128]{2,1,0:T(8,128)(2,1)S(1)} %bitcast.17, s32[1,1024]{1,0:T(1,128)S(1)} %get-tuple-element.13.limit_ref, ...), custom_call_target="tpu_custom_call" | custom-call | flops 2390753280 | bytes 1835008 | tf_op jit(solution)/shard_map/pallas_call | solution.py:150
  84.1 9.5 %all-to-all-done.2 = bf16[64,2,16,128]{3,2,1,0:T(8,128)(2,1)S(1)} async-done(((bf16[64,2,16,128]{3,2,1,0:T(8,128)(2,1)}), bf16[64,2,16,128]{3,2,1,0:T(8,128)(2,1)S(1)}, u32[]{:S(2)}, u32[]{:S(2)}) %all-to-all-start.2) | async-done | bytes 524320 | tf_op jit(solution)/shard_map/all_to_all | solution.py:320
  93.6 0.5 shard_map.90
  94.1 17.8 %all_to_all.21.parts_ref = bf16[16,64,128]{2,1,0:T(8,128)(2,1)S(1)} all-to-all(bf16[16,64,128]{2,1,0:T(8,128)(2,1)S(1)} %shard_map.90), channel_id=1, replica_groups=mesh['wide'=16,'tp'=64] {'wide'}, dimensions={0} | all-to-all | bytes 524288 | tf_op jit(solution)/shard_map/all_to_all | solution.py:322
  112.0 0.7 shard_map.91
  (1 shorter events, 0.0 us)
Async XLA Ops:
  0.6 0.7 copy-start
  1.4 28.4 %copy-start.1 = (s32[128,8]{0,1:T(8,128)S(1)}, s32[128,8]{0,1:T(8,128)}, u32[]{:S(2)}) copy-start(s32[128,8]{0,1:T(8,128)} %param.10) | copy-start | bytes 12292
  31.2 32.8 %copy-start.3 = (bf16[1,1,192,1024]{3,2,1,0:T(8,128)(2,1)S(1)}, bf16[1,1,192,1024]{3,2,1,0:T(8,128)(2,1)}, u32[]{:S(2)}) copy-start(bf16[1,1,192,1024]{3,2,1,0:T(8,128)(2,1)} %param.6) | copy-start | bytes 1179652
  31.2 32.8 %copy-start.4 = (bf16[1,1,192,1024]{3,2,1,0:T(8,128)(2,1)S(1)}, bf16[1,1,192,1024]{3,2,1,0:T(8,128)(2,1)}, u32[]{:S(2)}) copy-start(bf16[1,1,192,1024]{3,2,1,0:T(8,128)(2,1)} %param.11) | copy-start | bytes 1179652
  31.2 32.8 %copy-start.5 = (bf16[2,1,1,192,128]{4,3,2,1,0:T(8,128)(2,1)S(1)}, bf16[2,1,1,192,128]{4,3,2,1,0:T(8,128)(2,1)}, u32[]{:S(2)}) copy-start(bf16[2,1,1,192,128]{4,3,2,1,0:T(8,128)(2,1)} %param.7) | copy-start | bytes 294916
  31.2 32.8 %all-to-all-start.1 = ((bf16[64,2,16,128]{3,2,1,0:T(8,128)(2,1)}), bf16[64,2,16,128]{3,2,1,0:T(8,128)(2,1)S(1)}, u32[]{:S(2)}, u32[]{:S(2)}) async-start(bf16[64,2,16,128]{3,2,1,0:T(8,128)(2,1)} %bitcast.5), calls=%async_computation.1 | async-start | bytes 1048576 | tf_op jit(solution)/shard_map/all_to_all | solution.py:312
  45.8 0.7 copy-start.2
  70.3 23.3 %all-to-all-start.2 = ((bf16[64,2,16,128]{3,2,1,0:T(8,128)(2,1)}), bf16[64,2,16,128]{3,2,1,0:T(8,128)(2,1)S(1)}, u32[]{:S(2)}, u32[]{:S(2)}) async-start(bf16[64,2,16,128]{3,2,1,0:T(8,128)(2,1)} %get-tuple-element.18), calls=%async_computation.2 | async-start | bytes 1048576 | tf_op jit(solution)/shard_map/all_to_all | solution.py:320

commit v4 on v3

--- a/solution.py
+++ b/solution.py
@@ -103,7 +103,7 @@
         return q, g, w_doc_low, att, ds_doc, ds_own
 
 
-def limit_kernel(subs, kv_heads, ids_ref, lengths_ref, limit_ref):
+def limit_kernel(subs, kv_heads, after_ref, ids_ref, lengths_ref, limit_ref):
     limit_ref[...] = length_row(subs, kv_heads, limit_ref.shape[1], ids_ref, lengths_ref)
 
 
@@ -138,7 +138,7 @@
         rollout.unstack(dq_ref, first, (dq * rollout.scale).astype(jnp.bfloat16))
 
 
-def attention(q, g, own, ids, lengths, docs, subs, kv_heads):
+def attention(q, g, own, reads, ids, lengths, docs, subs, kv_heads):
     rows, width = q.shape
     head_dim = own.shape[2]
     slots = docs.size // (2 * head_dim)
@@ -162,7 +162,7 @@
         )(*args)
 
     row = jax.ShapeDtypeStruct((1, slots), jnp.int32)
-    limits = local(functools.partial(limit_kernel, subs, kv_heads), row, ids, lengths)
+    limits = local(functools.partial(limit_kernel, subs, kv_heads), row, reads, ids, lengths)
     d_docs, limits = call(
         functools.partial(document_kernel, uses),
         (jax.ShapeDtypeStruct(docs.shape, jnp.bfloat16), row),
@@ -205,8 +205,7 @@
     out_ref[...] = whole.reshape(out_ref.shape)
 
 
-def select_kernel(ids_ref, every_ref, out_ref, reads_ref, ids_out_ref, rows_ref):
-    ids_out_ref[...] = ids_ref[...]
+def select_kernel(ids_ref, every_ref, out_ref, reads_ref, rows_ref):
     owners, per_owner, head_dim = every_ref.shape
     subs, kv_heads, _, per_piece, _ = out_ref.shape
     uses = ids_ref.shape[0]
@@ -306,15 +305,15 @@
     flops = 2 * subs * uses * wide_width * docs_here * per_owner // docs_here * head_dim
 
     every = lax.all_to_all(local(slab_kernel, slabs, doc_kv), "wide", 0, 0, tiled=True)
-    picked, reads, ids = local(
-        select_kernel, (pieces, reads, jax.ShapeDtypeStruct(ids.shape, ids.dtype)), ids, every, scratch=(rows,), flops=flops
+    picked, reads = local(
+        select_kernel, (pieces, reads), ids, every, scratch=(rows,), flops=flops
     )
     docs = lax.all_to_all(
         picked.reshape(tp_width, 2, per_piece, head_dim), "tp", 0, 0, tiled=True
     )
 
     attended, d_query, ready, d_docs = attention(
-        queries[0, 0], d_out[0, 0], own_kv[:, 0, 0], ids, doc_lengths[None], docs, subs, kv_heads
+        queries[0, 0], d_out[0, 0], own_kv[:, 0, 0], reads, ids, doc_lengths[None], docs, subs, kv_heads
     )
 
     back = lax.all_to_all(d_docs, "tp", 0, 0, tiled=True).reshape(pieces.shape)

time: 113 us -> 113 us (level)
  no operation moved by 1% of the time
where the time goes in v4:
time: 113 us
  blocking collectives  46.3 us (41%)
  waiting for transfers between devices  26.9 us (24%)
  starting transfers between devices  21.2 us (19%)
  Pallas kernels  16.2 us (14%)
  local copies, waits for them, and re-layouts  1.38 us (1%)
    all_to_all x1, blocking collectives, shards(): lax.all_to_all(local(slab_kernel, slabs, doc_kv), 'wide', 0, 0, tiled=True)  28.4 us
    all_to_all x1, blocking collectives, shards(): parts = lax.all_to_all(by_doc, 'wide', 0, 0, tiled=True)  17.8 us
    all_to_all x1, waiting for transfers between devices, shards(): lax.all_to_all(picked.reshape(tp_width, 2, per_piece, head_dim), 'tp', 0,...  17.4 us
    all_to_all x1, starting transfers between devices, shards(): lax.all_to_all(picked.reshape(tp_width, 2, per_piece, head_dim), 'tp', 0,...  14.6 us
    pallas_call x2, Pallas kernels, call(): pl.pallas_call(kernel, out_shape=out, in_specs=[vmem] * len(args), out_sp...  13.5 us
    all_to_all x1, waiting for transfers between devices, shards(): back = lax.all_to_all(d_docs, 'tp', 0, 0, tiled=True).reshape(pieces.shape)  9.54 us
    all_to_all x1, starting transfers between devices, shards(): back = lax.all_to_all(d_docs, 'tp', 0, 0, tiled=True).reshape(pieces.shape)  6.6 us
    pallas_call x5, Pallas kernels, local(): pl.pallas_call(kernel, out_shape=out, in_specs=[vmem] * len(args), out_sp...  2.73 us
  transfers between devices with their start and end apart: 2, of which 2 were waited for; matrix products, arithmetic and copies ran while one was open for 0% of the time, Pallas kernels for 7%

profile of v4, /device:TPU:1, one launch (start us, length us, event | category | flops | bytes accessed | tf_op | source)
XLA Modules:
  0.0 112.6 jit_solution(15750894600934782086)
XLA Ops:
  0.6 0.0 copy-start.1
  0.6 0.7 copy-done.1
  1.3 0.1 shard_map.85
  1.4 0.0 copy-start
  1.4 28.4 %all_to_all.20.every_ref = bf16[16,64,128]{2,1,0:T(8,128)(2,1)S(1)} all-to-all(bf16[16,64,128]{2,1,0:T(8,128)(2,1)S(1)} %shard_map.85), channel_id=1, replica_groups=mesh['wide'=16,'tp'=64] {'wide'}, dimensions={0} | all-to-all | bytes 524288 | tf_op jit(solution)/shard_map/all_to_all | solution.py:307
  29.8 0.0 copy-done
  29.9 1.4 %shard_map.86 = (bf16[8,8,2,16,128]{4,3,2,1,0:T(8,128)(2,1)}, bf16[64,32]{1,0:T(8,128)(2,1)S(1)}) custom-call(s32[8,128]{1,0:T(8,128)S(1)} %bitcast.10, bf16[16,64,128]{2,1,0:T(8,128)(2,1)S(1)} %all_to_all.20.every_ref), custom_call_target="tpu_custom_call" | custom-call | flops 16777216 | bytes 532480 | tf_op jit(solution)/shard_map/pallas_call | solution.py:277
  31.2 0.0 copy-start.3
  31.2 0.0 copy-start.4
  31.2 14.6 %all-to-all-start.1 = ((bf16[64,2,16,128]{3,2,1,0:T(8,128)(2,1)}), bf16[64,2,16,128]{3,2,1,0:T(8,128)(2,1)S(1)}, u32[]{:S(2)}, u32[]{:S(2)}) async-start(bf16[64,2,16,128]{3,2,1,0:T(8,128)(2,1)} %bitcast.5), calls=%async_computation.1 | async-start | bytes 1048576 | tf_op jit(solution)/shard_map/all_to_all | solution.py:311
  45.8 0.0 copy-start.2
  45.8 0.6 copy-done.2
  46.5 0.2 shard_map.87.limit_ref
  46.7 17.4 %all-to-all-done.1.doc_ref = bf16[64,2,16,128]{3,2,1,0:T(8,128)(2,1)S(1)} async-done(((bf16[64,2,16,128]{3,2,1,0:T(8,128)(2,1)}), bf16[64,2,16,128]{3,2,1,0:T(8,128)(2,1)S(1)}, u32[]{:S(2)}, u32[]{:S(2)}) %all-to-all-start.1) | async-done | bytes 524320 | tf_op jit(solution)/shard_map/all_to_all | solution.py:311
  64.0 0.0 copy-done.3
  64.0 0.0 copy-done.4
  64.0 0.0 copy-done.5
  64.0 6.3 %shard_map.88 = (bf16[64,2,16,128]{3,2,1,0:T(8,128)(2,1)}, s32[1,1024]{1,0:T(1,128)S(1)}) custom-call(bf16[192,1024]{1,0:T(8,128)(2,1)S(1)} %bitcast.13, bf16[192,1024]{1,0:T(8,128)(2,1)S(1)} %bitcast.15, bf16[2,192,128]{2,1,0:T(8,128)(2,1)S(1)} %bitcast.17, s32[1,1024]{1,0:T(1,128)S(1)} %shard_map.87.limit_ref, ...), custom_call_target="tpu_custom_call" | custom-call | flops 2390753280 | bytes 1835008 | tf_op jit(solution)/shard_map/pallas_call | solution.py:150
  70.3 6.6 %all-to-all-start.2 = ((bf16[64,2,16,128]{3,2,1,0:T(8,128)(2,1)}), bf16[64,2,16,128]{3,2,1,0:T(8,128)(2,1)S(1)}, u32[]{:S(2)}, u32[]{:S(2)}) async-start(bf16[64,2,16,128]{3,2,1,0:T(8,128)(2,1)} %get-tuple-element.16), calls=%async_computation.2 | async-start | bytes 1048576 | tf_op jit(solution)/shard_map/all_to_all | solution.py:319
  76.9 7.2 %shard_map.89 = (bf16[192,1024]{1,0:T(8,128)(2,1)}, bf16[192,1024]{1,0:T(8,128)(2,1)}, s32[1,1024]{1,0:T(1,128)S(1)}) custom-call(bf16[192,1024]{1,0:T(8,128)(2,1)S(1)} %bitcast.14, bf16[192,1024]{1,0:T(8,128)(2,1)S(1)} %bitcast.16, bf16[2,192,128]{2,1,0:T(8,128)(2,1)S(1)} %bitcast.18, s32[1,1024]{1,0:T(1,128)S(1)} %get-tuple-element.12.limit_ref, ...), custom_call_target="tpu_custom_call" | custom-call | flops 2390753280 | bytes 1835008 | tf_op jit(solution)/shard_map/pallas_call | solution.py:150
  84.1 9.5 %all-to-all-done.2 = bf16[64,2,16,128]{3,2,1,0:T(8,128)(2,1)S(1)} async-done(((bf16[64,2,16,128]{3,2,1,0:T(8,128)(2,1)}), bf16[64,2,16,128]{3,2,1,0:T(8,128)(2,1)S(1)}, u32[]{:S(2)}, u32[]{:S(2)}) %all-to-all-start.2) | async-done | bytes 524320 | tf_op jit(solution)/shard_map/all_to_all | solution.py:319
  93.6 0.5 shard_map.90
  94.1 17.8 %all_to_all.21.parts_ref = bf16[16,64,128]{2,1,0:T(8,128)(2,1)S(1)} all-to-all(bf16[16,64,128]{2,1,0:T(8,128)(2,1)S(1)} %shard_map.90), channel_id=1, replica_groups=mesh['wide'=16,'tp'=64] {'wide'}, dimensions={0} | all-to-all | bytes 524288 | tf_op jit(solution)/shard_map/all_to_all | solution.py:321
  112.0 0.7 shard_map.91
  (1 shorter events, 0.0 us)
Async XLA Ops:
  0.6 0.7 copy-start.1
  1.4 28.4 %copy-start = (s32[128,8]{0,1:T(8,128)S(1)}, s32[128,8]{0,1:T(8,128)}, u32[]{:S(2)}) copy-start(s32[128,8]{0,1:T(8,128)} %param.10) | copy-start | bytes 12292
  31.2 32.8 %copy-start.3 = (bf16[1,1,192,1024]{3,2,1,0:T(8,128)(2,1)S(1)}, bf16[1,1,192,1024]{3,2,1,0:T(8,128)(2,1)}, u32[]{:S(2)}) copy-start(bf16[1,1,192,1024]{3,2,1,0:T(8,128)(2,1)} %param.6) | copy-start | bytes 1179652
  31.2 32.8 %copy-start.4 = (bf16[1,1,192,1024]{3,2,1,0:T(8,128)(2,1)S(1)}, bf16[1,1,192,1024]{3,2,1,0:T(8,128)(2,1)}, u32[]{:S(2)}) copy-start(bf16[1,1,192,1024]{3,2,1,0:T(8,128)(2,1)} %param.11) | copy-start | bytes 1179652
  31.2 32.8 %copy-start.5 = (bf16[2,1,1,192,128]{4,3,2,1,0:T(8,128)(2,1)S(1)}, bf16[2,1,1,192,128]{4,3,2,1,0:T(8,128)(2,1)}, u32[]{:S(2)}) copy-start(bf16[2,1,1,192,128]{4,3,2,1,0:T(8,128)(2,1)} %param.7) | copy-start | bytes 294916
  31.2 32.8 %all-to-all-start.1 = ((bf16[64,2,16,128]{3,2,1,0:T(8,128)(2,1)}), bf16[64,2,16,128]{3,2,1,0:T(8,128)(2,1)S(1)}, u32[]{:S(2)}, u32[]{:S(2)}) async-start(bf16[64,2,16,128]{3,2,1,0:T(8,128)(2,1)} %bitcast.5), calls=%async_computation.1 | async-start | bytes 1048576 | tf_op jit(solution)/shard_map/all_to_all | solution.py:311
  45.8 0.7 copy-start.2
  70.3 23.3 %all-to-all-start.2 = ((bf16[64,2,16,128]{3,2,1,0:T(8,128)(2,1)}), bf16[64,2,16,128]{3,2,1,0:T(8,128)(2,1)S(1)}, u32[]{:S(2)}, u32[]{:S(2)}) async-start(bf16[64,2,16,128]{3,2,1,0:T(8,128)(2,1)} %get-tuple-element.16), calls=%async_computation.2 | async-start | bytes 1048576 | tf_op jit(solution)/shard_map/all_to_all | solution.py:319

commit v5 on v2

--- a/solution.py
+++ b/solution.py
@@ -12,7 +12,8 @@
 NN = (((1,), (0,)), ((), ()))
 TN = (((0,), (0,)), ((), ()))
 OUT_OF_REACH = -2e38
-STACK = 4
+DOCUMENT_STACK = 8
+QUERY_STACK = 4
 VMEM_BYTES = 48 * 1024 * 1024
 
 
@@ -41,7 +42,8 @@
 
 
 class Rollout:
-    def __init__(self, uses, q_ref, g_ref, own_ref, doc_ref, limits):
+    def __init__(self, stack, uses, q_ref, g_ref, own_ref, doc_ref, limits):
+        self.stack = stack
         self.q_ref, self.g_ref = q_ref, g_ref
         sources, _, per_source, self.head_dim = doc_ref.shape
         self.rows = q_ref.shape[0]
@@ -57,19 +59,19 @@
         causal = lax.broadcasted_iota(jnp.int32, square, 1) <= lax.broadcasted_iota(
             jnp.int32, square, 0
         )
-        self.causal = jnp.concatenate([causal.astype(jnp.int32)] * STACK, axis=0) > 0
+        self.causal = jnp.concatenate([causal.astype(jnp.int32)] * stack, axis=0) > 0
 
     def stacked(self, ref, first):
         return jnp.concatenate(
             [
                 ref[:, pl.ds((first + h) * self.head_dim, self.head_dim)]
-                for h in range(STACK)
+                for h in range(self.stack)
             ],
             axis=0,
         )
 
     def unstack(self, ref, first, value):
-        for h in range(STACK):
+        for h in range(self.stack):
             ref[:, pl.ds((first + h) * self.head_dim, self.head_dim)] = value[
                 h * self.rows : (h + 1) * self.rows
             ]
@@ -108,13 +110,13 @@
     sources, _, per_source, head_dim = doc_ref.shape
     limits = length_row(subs, kv_heads, sources * per_source, ids_ref, lengths_ref)
     limit_ref[...] = limits
-    rollout = Rollout(ids_ref.shape[0], q_ref, g_ref, own_ref, doc_ref, limits)
-    for first in range(0, rollout.heads, STACK):
+    rollout = Rollout(DOCUMENT_STACK, ids_ref.shape[0], q_ref, g_ref, own_ref, doc_ref, limits)
+    for first in range(0, rollout.heads, rollout.stack):
         q, g, w_doc, _, ds_doc, _ = rollout.heads_from(first)
         dk, dv = dot(q.T, ds_doc, NN), dot(g.T, w_doc, NN)
         if first:
             dk, dv = dk_sum[...] + dk, dv_sum[...] + dv
-        if first + STACK < rollout.heads:
+        if first + rollout.stack < rollout.heads:
             dk_sum[...] = dk
             dv_sum[...] = dv
         else:
@@ -125,8 +127,8 @@
 
 def query_kernel(uses, q_ref, g_ref, own_ref, limit_ref, doc_ref, att_ref, dq_ref, ready_ref):
     ready_ref[...] = limit_ref[...]
-    rollout = Rollout(uses, q_ref, g_ref, own_ref, doc_ref, limit_ref[...])
-    for first in range(0, rollout.heads, STACK):
+    rollout = Rollout(QUERY_STACK, uses, q_ref, g_ref, own_ref, doc_ref, limit_ref[...])
+    for first in range(0, rollout.heads, rollout.stack):
         _, _, _, att, ds_doc, ds_own = rollout.heads_from(first)
         dq = dot(ds_doc, rollout.doc_k, NN) + dot(ds_own(), rollout.own_k, NN)
         rollout.unstack(att_ref, first, att)

time: 113 us -> 113 us (level)
  no operation moved by 1% of the time
where the time goes in v5:
time: 113 us; the launch traced here: 112 us
  blocking collectives  78.9 us (70%)
  Pallas kernels  15.2 us (13%)
  waiting for transfers between devices  9.54 us (8%)
  starting transfers between devices  6.61 us (6%)
  local copies, waits for them, and re-layouts  1.38 us (1%)
    all_to_all x1, blocking collectives, shards(): lax.all_to_all(picked.reshape(tp_width, 2, per_piece, head_dim), 'tp', 0,...  32.6 us
    all_to_all x1, blocking collectives, shards(): lax.all_to_all(local(slab_kernel, slabs, doc_kv), 'wide', 0, 0, tiled=True)  28.4 us
    all_to_all x1, blocking collectives, shards(): parts = lax.all_to_all(by_doc, 'wide', 0, 0, tiled=True)  17.8 us
    pallas_call x2, Pallas kernels, call(): pl.pallas_call(kernel, out_shape=out, in_specs=[vmem] * len(args), out_sp...  13.5 us
    all_to_all x1, waiting for transfers between devices, shards(): back = lax.all_to_all(d_docs, 'tp', 0, 0, tiled=True).reshape(pieces.shape)  9.54 us
    all_to_all x1, starting transfers between devices, shards(): back = lax.all_to_all(d_docs, 'tp', 0, 0, tiled=True).reshape(pieces.shape)  6.61 us
  transfers between devices with their start and end apart: 1, of which 1 were waited for; matrix products, arithmetic and copies ran while one was open for 0% of the time, Pallas kernels for 6%

profile of v5, /device:TPU:1, one launch (start us, length us, event | category | flops | bytes accessed | tf_op | source)
XLA Modules:
  0.0 112.3 jit_solution(15563034411512161947)
XLA Ops:
  0.6 0.0 copy-start
  0.6 0.7 copy-done
  1.3 0.1 shard_map.85
  1.4 0.0 copy-start.1
  1.4 28.4 %all_to_all.20.every_ref = bf16[16,64,128]{2,1,0:T(8,128)(2,1)S(1)} all-to-all(bf16[16,64,128]{2,1,0:T(8,128)(2,1)S(1)} %shard_map.85), channel_id=1, replica_groups=mesh['wide'=16,'tp'=64] {'wide'}, dimensions={0} | all-to-all | bytes 524288 | tf_op jit(solution)/shard_map/all_to_all | solution.py:306
  29.8 0.0 copy-done.1
  29.9 0.5 shard_map.86
  30.4 0.0 copy-start.2
  30.4 0.0 copy-start.3
  30.4 0.0 copy-start.4
  30.4 32.6 %all_to_all.21.doc_ref = bf16[64,2,16,128]{3,2,1,0:T(8,128)(2,1)S(1)} all-to-all(bf16[64,2,16,128]{3,2,1,0:T(8,128)(2,1)S(1)} %bitcast.10), channel_id=1, replica_groups=mesh['wide'=16,'tp'=64] {'tp'}, dimensions={0} | all-to-all | bytes 1048576 | tf_op jit(solution)/shard_map/all_to_all | solution.py:310
  63.0 0.0 copy-start.5
  63.0 0.0 copy-done.2
  63.0 0.0 copy-done.3
  63.0 0.0 copy-done.4
  63.0 0.6 copy-done.5
  63.7 6.3 %shard_map.87 = (bf16[64,2,16,128]{3,2,1,0:T(8,128)(2,1)}, s32[1,1024]{1,0:T(1,128)S(1)}) custom-call(bf16[192,1024]{1,0:T(8,128)(2,1)S(1)} %bitcast.13, bf16[192,1024]{1,0:T(8,128)(2,1)S(1)} %bitcast.15, bf16[2,192,128]{2,1,0:T(8,128)(2,1)S(1)} %bitcast.17, s32[8,128]{1,0:T(8,128)S(1)} %bitcast.12, s32[1,32]{1,0:T(1,128)S(1)} %bitcast.19, ...), custom_call_target="tpu_custom_call" | custom-call | flops 2390753280 | bytes 1835008 | tf_op jit(solution)/shard_map/pallas_call | solution.py:147
  69.9 6.6 %all-to-all-start.2 = ((bf16[64,2,16,128]{3,2,1,0:T(8,128)(2,1)}), bf16[64,2,16,128]{3,2,1,0:T(8,128)(2,1)S(1)}, u32[]{:S(2)}, u32[]{:S(2)}) async-start(bf16[64,2,16,128]{3,2,1,0:T(8,128)(2,1)} %get-tuple-element.16), calls=%async_computation.2 | async-start | bytes 1048576 | tf_op jit(solution)/shard_map/all_to_all | solution.py:318
  76.5 7.2 %shard_map.88 = (bf16[192,1024]{1,0:T(8,128)(2,1)}, bf16[192,1024]{1,0:T(8,128)(2,1)}, s32[1,1024]{1,0:T(1,128)S(1)}) custom-call(bf16[192,1024]{1,0:T(8,128)(2,1)S(1)} %bitcast.14, bf16[192,1024]{1,0:T(8,128)(2,1)S(1)} %bitcast.16, bf16[2,192,128]{2,1,0:T(8,128)(2,1)S(1)} %bitcast.18, s32[1,1024]{1,0:T(1,128)S(1)} %get-tuple-element.11.limit_ref, ...), custom_call_target="tpu_custom_call" | custom-call | flops 2390753280 | bytes 1835008 | tf_op jit(solution)/shard_map/pallas_call | solution.py:147
  83.7 9.5 %all-to-all-done.2 = bf16[64,2,16,128]{3,2,1,0:T(8,128)(2,1)S(1)} async-done(((bf16[64,2,16,128]{3,2,1,0:T(8,128)(2,1)}), bf16[64,2,16,128]{3,2,1,0:T(8,128)(2,1)S(1)}, u32[]{:S(2)}, u32[]{:S(2)}) %all-to-all-start.2) | async-done | bytes 524320 | tf_op jit(solution)/shard_map/all_to_all | solution.py:318
  93.3 0.5 shard_map.89
  93.8 17.8 %all_to_all.22.parts_ref = bf16[16,64,128]{2,1,0:T(8,128)(2,1)S(1)} all-to-all(bf16[16,64,128]{2,1,0:T(8,128)(2,1)S(1)} %shard_map.89), channel_id=1, replica_groups=mesh['wide'=16,'tp'=64] {'wide'}, dimensions={0} | all-to-all | bytes 524288 | tf_op jit(solution)/shard_map/all_to_all | solution.py:320
  111.6 0.7 shard_map.90
Async XLA Ops:
  0.6 0.7 copy-start
  1.4 28.4 %copy-start.1 = (s32[128,8]{0,1:T(8,128)S(1)}, s32[128,8]{0,1:T(8,128)}, u32[]{:S(2)}) copy-start(s32[128,8]{0,1:T(8,128)} %param.10) | copy-start | bytes 12292
  30.4 32.6 %copy-start.2 = (bf16[1,1,192,1024]{3,2,1,0:T(8,128)(2,1)S(1)}, bf16[1,1,192,1024]{3,2,1,0:T(8,128)(2,1)}, u32[]{:S(2)}) copy-start(bf16[1,1,192,1024]{3,2,1,0:T(8,128)(2,1)} %param.6) | copy-start | bytes 1179652
  30.4 32.6 %copy-start.3 = (bf16[1,1,192,1024]{3,2,1,0:T(8,128)(2,1)S(1)}, bf16[1,1,192,1024]{3,2,1,0:T(8,128)(2,1)}, u32[]{:S(2)}) copy-start(bf16[1,1,192,1024]{3,2,1,0:T(8,128)(2,1)} %param.11) | copy-start | bytes 1179652
  30.4 32.6 %copy-start.4 = (bf16[2,1,1,192,128]{4,3,2,1,0:T(8,128)(2,1)S(1)}, bf16[2,1,1,192,128]{4,3,2,1,0:T(8,128)(2,1)}, u32[]{:S(2)}) copy-start(bf16[2,1,1,192,128]{4,3,2,1,0:T(8,128)(2,1)} %param.7) | copy-start | bytes 294916
  63.0 0.7 copy-start.5
  69.9 23.3 %all-to-all-start.2 = ((bf16[64,2,16,128]{3,2,1,0:T(8,128)(2,1)}), bf16[64,2,16,128]{3,2,1,0:T(8,128)(2,1)S(1)}, u32[]{:S(2)}, u32[]{:S(2)}) async-start(bf16[64,2,16,128]{3,2,1,0:T(8,128)(2,1)} %get-tuple-element.16), calls=%async_computation.2 | async-start | bytes 1048576 | tf_op jit(solution)/shard_map/all_to_all | solution.py:318

commit v6 on v5

--- a/solution.py
+++ b/solution.py
@@ -31,9 +31,12 @@
 
 def length_row(subs, kv_heads, slots, ids_ref, lengths_ref):
     mine = documents(ids_ref, subs, lax.axis_index("tp") // kv_heads)
-    uses, docs = ids_ref.shape[0], lengths_ref.shape[1]
+    uses, docs = ids_ref.shape[0], lengths_ref.shape[0]
     column = lax.broadcasted_iota(jnp.int32, (uses, docs), 1)
-    lengths = jnp.where(mine == column, lengths_ref[...].astype(jnp.float32), 0.0)
+    lengths = jnp.zeros((uses, docs), jnp.int32)
+    for doc in range(docs):
+        lengths = jnp.where(column == doc, lengths_ref[doc], lengths)
+    lengths = jnp.where(mine == column, lengths.astype(jnp.float32), 0.0)
     lengths = jnp.sum(lengths, axis=1, keepdims=True)
     use = lax.broadcasted_iota(jnp.int32, (uses, 128), 0)
     lane = lax.broadcasted_iota(jnp.int32, (uses, 128), 1)
@@ -141,13 +144,14 @@
     slots = docs.size // (2 * head_dim)
     uses = ids.shape[0]
     vmem = pl.BlockSpec(memory_space=pltpu.VMEM)
+    smem = pl.BlockSpec(memory_space=pltpu.SMEM)
     pairs = width // head_dim * rows * (slots + rows)
 
     def call(kernel, out, *args, scratch=()):
         return pl.pallas_call(
             kernel,
             out_shape=out,
-            in_specs=[vmem] * len(args),
+            in_specs=[smem if x is lengths else vmem for x in args],
             out_specs=(vmem,) * len(out),
             scratch_shapes=list(scratch),
             compiler_params=pltpu.CompilerParams(vmem_limit_bytes=VMEM_BYTES),
@@ -312,7 +316,7 @@
     )
 
     attended, d_query, ready, d_docs = attention(
-        queries[0, 0], d_out[0, 0], own_kv[:, 0, 0], ids, doc_lengths[None], docs, subs, kv_heads
+        queries[0, 0], d_out[0, 0], own_kv[:, 0, 0], ids, doc_lengths, docs, subs, kv_heads
     )
 
     back = lax.all_to_all(d_docs, "tp", 0, 0, tiled=True).reshape(pieces.shape)

time: 113 us -> 113 us (level)
  no operation moved by 1% of the time
where the time goes in v6:
time: 113 us
  blocking collectives  78.8 us (70%)
  Pallas kernels  15.7 us (14%)
  waiting for transfers between devices  9.56 us (8%)
  starting transfers between devices  6.61 us (6%)
  local copies, waits for them, and re-layouts  1.38 us (1%)
    all_to_all x1, blocking collectives, shards(): lax.all_to_all(picked.reshape(tp_width, 2, per_piece, head_dim), 'tp', 0,...  32.6 us
    all_to_all x1, blocking collectives, shards(): lax.all_to_all(local(slab_kernel, slabs, doc_kv), 'wide', 0, 0, tiled=True)  28.4 us
    all_to_all x1, blocking collectives, shards(): parts = lax.all_to_all(by_doc, 'wide', 0, 0, tiled=True)  17.8 us
    pallas_call x2, Pallas kernels, call(): pl.pallas_call(kernel, out_shape=out, in_specs=[smem if x is lengths else...  14 us
    all_to_all x1, waiting for transfers between devices, shards(): back = lax.all_to_all(d_docs, 'tp', 0, 0, tiled=True).reshape(pieces.shape)  9.56 us
    all_to_all x1, starting transfers between devices, shards(): back = lax.all_to_all(d_docs, 'tp', 0, 0, tiled=True).reshape(pieces.shape)  6.61 us
  transfers between devices with their start and end apart: 1, of which 1 were waited for; matrix products, arithmetic and copies ran while one was open for 0% of the time, Pallas kernels for 6%

profile of v6, /device:TPU:1, one launch (start us, length us, event | category | flops | bytes accessed | tf_op | source)
XLA Modules:
  0.0 112.8 jit_solution(762243635063545777)
XLA Ops:
  0.6 0.0 copy-start
  0.6 0.7 copy-done
  1.3 0.1 shard_map.85
  1.4 0.0 copy-start.1
  1.4 28.4 %all_to_all.20.every_ref = bf16[16,64,128]{2,1,0:T(8,128)(2,1)S(1)} all-to-all(bf16[16,64,128]{2,1,0:T(8,128)(2,1)S(1)} %shard_map.85), channel_id=1, replica_groups=mesh['wide'=16,'tp'=64] {'wide'}, dimensions={0} | all-to-all | bytes 524288 | tf_op jit(solution)/shard_map/all_to_all | solution.py:310
  29.8 0.0 copy-done.1
  29.9 0.5 shard_map.86
  30.4 0.0 copy-start.2
  30.4 0.0 copy-start.3
  30.4 0.0 copy-start.4
  30.4 32.6 %all_to_all.21.doc_ref = bf16[64,2,16,128]{3,2,1,0:T(8,128)(2,1)S(1)} all-to-all(bf16[64,2,16,128]{3,2,1,0:T(8,128)(2,1)S(1)} %bitcast.9), channel_id=1, replica_groups=mesh['wide'=16,'tp'=64] {'tp'}, dimensions={0} | all-to-all | bytes 1048576 | tf_op jit(solution)/shard_map/all_to_all | solution.py:314
  63.0 0.0 copy-start.5
  63.0 0.0 copy-done.2
  63.0 0.0 copy-done.3
  63.0 0.0 copy-done.4
  63.0 0.6 copy-done.5
  63.7 6.8 %shard_map.87 = (bf16[64,2,16,128]{3,2,1,0:T(8,128)(2,1)}, s32[1,1024]{1,0:T(1,128)S(1)}) custom-call(bf16[192,1024]{1,0:T(8,128)(2,1)S(1)} %bitcast.12, bf16[192,1024]{1,0:T(8,128)(2,1)S(1)} %bitcast.14, bf16[2,192,128]{2,1,0:T(8,128)(2,1)S(1)} %bitcast.16, s32[8,128]{1,0:T(8,128)S(1)} %bitcast.11, s32[32]{0:T(128)S(1)} %copy-done.5, ...), custom_call_target="tpu_custom_call" | custom-call | flops 2390753280 | bytes 1835008 | tf_op jit(solution)/shard_map/pallas_call | solution.py:151
  70.5 6.6 %all-to-all-start.2 = ((bf16[64,2,16,128]{3,2,1,0:T(8,128)(2,1)}), bf16[64,2,16,128]{3,2,1,0:T(8,128)(2,1)S(1)}, u32[]{:S(2)}, u32[]{:S(2)}) async-start(bf16[64,2,16,128]{3,2,1,0:T(8,128)(2,1)} %get-tuple-element.16), calls=%async_computation.2 | async-start | bytes 1048576 | tf_op jit(solution)/shard_map/all_to_all | solution.py:322
  77.1 7.2 %shard_map.88 = (bf16[192,1024]{1,0:T(8,128)(2,1)}, bf16[192,1024]{1,0:T(8,128)(2,1)}, s32[1,1024]{1,0:T(1,128)S(1)}) custom-call(bf16[192,1024]{1,0:T(8,128)(2,1)S(1)} %bitcast.13, bf16[192,1024]{1,0:T(8,128)(2,1)S(1)} %bitcast.15, bf16[2,192,128]{2,1,0:T(8,128)(2,1)S(1)} %bitcast.17, s32[1,1024]{1,0:T(1,128)S(1)} %get-tuple-element.11.limit_ref, ...), custom_call_target="tpu_custom_call" | custom-call | flops 2390753280 | bytes 1835008 | tf_op jit(solution)/shard_map/pallas_call | solution.py:151
  84.3 9.6 %all-to-all-done.2 = bf16[64,2,16,128]{3,2,1,0:T(8,128)(2,1)S(1)} async-done(((bf16[64,2,16,128]{3,2,1,0:T(8,128)(2,1)}), bf16[64,2,16,128]{3,2,1,0:T(8,128)(2,1)S(1)}, u32[]{:S(2)}, u32[]{:S(2)}) %all-to-all-start.2) | async-done | bytes 524320 | tf_op jit(solution)/shard_map/all_to_all | solution.py:322
  93.8 0.5 shard_map.89
  94.3 17.8 %all_to_all.22.parts_ref = bf16[16,64,128]{2,1,0:T(8,128)(2,1)S(1)} all-to-all(bf16[16,64,128]{2,1,0:T(8,128)(2,1)S(1)} %shard_map.89), channel_id=1, replica_groups=mesh['wide'=16,'tp'=64] {'wide'}, dimensions={0} | all-to-all | bytes 524288 | tf_op jit(solution)/shard_map/all_to_all | solution.py:324
  112.2 0.7 shard_map.90
Async XLA Ops:
  0.6 0.7 copy-start
  1.4 28.4 %copy-start.1 = (s32[128,8]{0,1:T(8,128)S(1)}, s32[128,8]{0,1:T(8,128)}, u32[]{:S(2)}) copy-start(s32[128,8]{0,1:T(8,128)} %param.10) | copy-start | bytes 12292
  30.4 32.6 %copy-start.2 = (bf16[1,1,192,1024]{3,2,1,0:T(8,128)(2,1)S(1)}, bf16[1,1,192,1024]{3,2,1,0:T(8,128)(2,1)}, u32[]{:S(2)}) copy-start(bf16[1,1,192,1024]{3,2,1,0:T(8,128)(2,1)} %param.6) | copy-start | bytes 1179652
  30.4 32.6 %copy-start.3 = (bf16[1,1,192,1024]{3,2,1,0:T(8,128)(2,1)S(1)}, bf16[1,1,192,1024]{3,2,1,0:T(8,128)(2,1)}, u32[]{:S(2)}) copy-start(bf16[1,1,192,1024]{3,2,1,0:T(8,128)(2,1)} %param.11) | copy-start | bytes 1179652
  30.4 32.6 %copy-start.4 = (bf16[2,1,1,192,128]{4,3,2,1,0:T(8,128)(2,1)S(1)}, bf16[2,1,1,192,128]{4,3,2,1,0:T(8,128)(2,1)}, u32[]{:S(2)}) copy-start(bf16[2,1,1,192,128]{4,3,2,1,0:T(8,128)(2,1)} %param.7) | copy-start | bytes 294916
  63.0 0.7 copy-start.5
  70.5 23.4 %all-to-all-start.2 = ((bf16[64,2,16,128]{3,2,1,0:T(8,128)(2,1)}), bf16[64,2,16,128]{3,2,1,0:T(8,128)(2,1)S(1)}, u32[]{:S(2)}, u32[]{:S(2)}) async-start(bf16[64,2,16,128]{3,2,1,0:T(8,128)(2,1)} %get-tuple-element.16), calls=%async_computation.2 | async-start | bytes 1048576 | tf_op jit(solution)/shard_map/all_to_all | solution.py:322
